TPU v7x, 32 devices: a whole 2x2x4 slice. The times are simulated.
32 devices in a mesh: src: 4 (over y, x), rcv: 4 (over z), seg: 2 (over core).
Axes of the slice: x: 2, y: 2, z: 4, core: 2. Of those that a mesh axis runs over, the one named last changes fastest.
Arguments:
- traces: bfloat16 [4, 512, 512], P('seg', 'src'), may hold values from -6 to 6
- fir_taps: bfloat16 [31], replicated, may hold values from -1 to 1
- pair_bins: int32 [512, 512], P('src', 'rcv'), may hold values from 0 to 1023, as said below
- bin_order: int32 [1024], replicated, may hold values from 0 to 1023, as said below
Outputs:
- owned_stacks: float32 [1024, 128], P(('src', 'rcv', 'seg'))
Inputs may be any that keep to these rules, and one draw needn't show every extreme that they name: pair_bins[a, b] = floor((p_b - p_a) / 2) + 512 for channel positions p_c = 2 * c + e_c with e_c in 0 or 1, e of the first channel 0 and of the last 1; so pair_bins[a, b] is b - a + 511 or b - a + 512. bin_order holds every bin once; for every owner q the bins in rows q * 32 to (q + 1) * 32 - 1 are all congruent modulo 32.
All inputs are finite; a program needn't handle non-finite values.
Results may differ from a plain program's by a relative error of at most 0.0012.
Values may be sent and summed in bfloat16 or wider, within the bound.
No kernel may reach another device: no remote copies, remote signals or barrier semaphores. Data moves between devices by JAX's collectives and lax.ppermute only.
A program may use at most 64 MiB of HBM per device.

v0:
```python
import jax
import jax.numpy as jnp
from jax import lax
from jax.sharding import PartitionSpec as P

MAXLAG = 64


def broadcast(block, axis, holder):
    block = jnp.where(lax.axis_index(axis) == holder, block, jnp.zeros_like(block))
    return lax.psum(block, axis)


def fir_matrix(fir_taps, length):
    column = jnp.arange(length)[None, :]
    row_index = jnp.arange(length)[:, None]
    offset = column - row_index + fir_taps.shape[0] // 2
    matrix = jnp.zeros((length, length), jnp.float32)
    for tap_index in range(fir_taps.shape[0]):
        matrix = matrix + jnp.where(
            offset == tap_index, fir_taps[tap_index].astype(jnp.float32), jnp.float32(0.0)
        )
    return matrix.astype(fir_taps.dtype)


def filter_rows(trace_rows, matrix):
    flattened = trace_rows.reshape(-1, trace_rows.shape[-1])
    product = jnp.dot(flattened, matrix, preferred_element_type=jnp.float32)
    return product.astype(jnp.bfloat16).reshape(trace_rows.shape)


def skew_sum(block):
    rows, width, depth = block.shape
    padded = jnp.pad(block, ((0, 0), (0, rows), (0, 0)))
    flat = padded.reshape(rows * (width + rows), depth)[: rows * (width + rows - 1)]
    return flat.reshape(rows, width + rows - 1, depth).sum(axis=0)


def on_device(traces, fir_taps, pair_bins, bin_order):
    seg_local, block_width, length = traces.shape
    src_count = lax.axis_size("src")
    rcv_count = lax.axis_size("rcv")
    seg_count = lax.axis_size("seg")
    bin_count = bin_order.shape[0]
    lag_count = 2 * MAXLAG
    matrix = fir_matrix(fir_taps, length)
    source = filter_rows(traces, matrix)
    receiver = broadcast(source, "src", lax.axis_index("rcv"))
    padded = jnp.pad(receiver, ((0, 0), (0, 0), (MAXLAG, MAXLAG - 1)))
    channel_count = block_width * src_count
    window_base = (
        (lax.axis_index("rcv") - lax.axis_index("src")) * block_width + channel_count - block_width
    )
    window_rows = 2 * block_width
    local_bins = pair_bins - window_base
    block_rows = min(32, block_width)
    turn_count = block_width // block_rows
    column = jnp.arange(block_width, dtype=jnp.int32)[None, :]
    row_steps = jnp.arange(block_rows, dtype=jnp.int32)[:, None]

    def one_turn(turn_index, running):
        first_row = turn_index * block_rows
        rows = jnp.flip(lax.dynamic_slice_in_dim(source, first_row, block_rows, 1), 1)
        values = lax.conv_general_dilated(
            padded,
            rows,
            (1,),
            "VALID",
            dimension_numbers=("CNH", "IOH", "CNH"),
            preferred_element_type=jnp.float32,
        )
        labels = jnp.flip(lax.dynamic_slice_in_dim(local_bins, first_row, block_rows, 0), 0)
        offset = block_width - block_rows - first_row
        place = column + row_steps + offset
        upper = (labels - place).astype(jnp.float32)[:, :, None]
        upper_part = values * upper
        summed = skew_sum(jnp.concatenate([values - upper_part, upper_part], axis=2))
        current = lax.dynamic_slice_in_dim(running, offset, summed.shape[0], 0)
        return lax.dynamic_update_slice_in_dim(running, current + summed, offset, 0)

    start_sums = jnp.zeros((window_rows, 2 * lag_count), jnp.float32)
    running = lax.fori_loop(0, turn_count, one_turn, start_sums)
    window_sums = running[:, :lag_count] + jnp.pad(running[:-1, lag_count:], ((1, 0), (0, 0)))
    all_place = column + jnp.arange(block_width, dtype=jnp.int32)[:, None]
    upper_all = (jnp.flip(local_bins, 0) - all_place).astype(jnp.float32)
    masks = jnp.stack([1.0 - upper_all, upper_all], axis=2) / seg_count
    count_pair = skew_sum(masks)
    window_counts = jnp.pad(count_pair[:, 0], (0, 1)) + jnp.pad(count_pair[:, 1], (1, 0))
    owner_count = src_count * rcv_count * seg_count
    per_owner = bin_count // owner_count
    depth = (window_rows + 2 * owner_count - 2) // owner_count
    start_block = window_base // owner_count
    lead = window_base - start_block * owner_count
    spread = lax.dynamic_update_slice_in_dim(
        jnp.zeros((depth * owner_count, lag_count), jnp.float32), window_sums, lead, 0
    )
    spread_counts = lax.dynamic_update_slice_in_dim(
        jnp.zeros((depth * owner_count,), jnp.float32), window_counts, lead, 0
    )
    residues = bin_order.reshape(owner_count, per_owner)[:, 0] % owner_count
    outgoing = jnp.take(spread.reshape(depth, owner_count, lag_count), residues, axis=1)
    outgoing_counts = jnp.take(spread_counts.reshape(depth, owner_count), residues, axis=1)
    incoming, incoming_counts = (
        lax.all_to_all(outgoing, ("src", "rcv", "seg"), split_axis=1, concat_axis=1, tiled=True),
        lax.all_to_all(
            outgoing_counts, ("src", "rcv", "seg"), split_axis=1, concat_axis=1, tiled=True
        ),
    )
    sender = jnp.arange(owner_count, dtype=jnp.int32)
    sender_src = sender // (rcv_count * seg_count)
    sender_rcv = sender // seg_count % rcv_count
    sender_start = (
        (sender_rcv - sender_src) * block_width + channel_count - block_width
    ) // owner_count
    target = sender_start[None, :] + jnp.arange(depth, dtype=jnp.int32)[:, None]
    my_rows = (
        lax.dynamic_slice_in_dim(
            bin_order, lax.axis_index(("src", "rcv", "seg")) * per_owner, per_owner, 0
        )
        // owner_count
    )
    select = (target[:, :, None] == my_rows[None, None, :]).astype(jnp.float32)
    owned_sums = jnp.einsum("udl,udp->pl", incoming, select, precision=lax.Precision.HIGHEST)
    owned_counts = jnp.einsum("ud,udp->p", incoming_counts, select, precision=lax.Precision.HIGHEST)
    normalizer = lax.rsqrt(jnp.maximum(owned_counts, 1.0) * (seg_local * seg_count * length))
    return owned_sums * normalizer[:, None]


def solution(mesh):
    return jax.shard_map(
        on_device,
        mesh=mesh,
        in_specs=(P("seg", "src", None), P(), P("src", "rcv"), P()),
        out_specs=P(("src", "rcv", "seg"), None),
        check_vma=False,
    )
```

profile of v0, /device:TPU:0, one launch (start us, length us, event | category | flops | bytes accessed | tf_op | source)
XLA Modules:
  0.0 266.2 jit_solution(107821025378856457)
XLA Ops:
  6.5 0.9 reverse.3
  10.9 7.3 %all-to-all-start.1 = ((f32[9,32,1]{0,2,1:T(1,128)}), f32[9,32,1]{0,2,1:T(1,128)S(1)}, u32[]{:S(2)}, u32[]{:S(2)}) async-start(f32[9,32,1]{0,2,1:T(1,128)} %bitcast.44), calls=%async_computation.1 | async-start | bytes 32768 | tf_op jit(solution)/shard_map/all_to_all | solution.py:105
  18.2 2.1 fusion.152
  20.3 1.8 fusion.153
  41.6 4.0 %convolution_convert_fusion = bf16[512,256]{0,1:T(8,128)(2,1)S(1)} fusion(bf16[256,512]{1,0:T(8,128)(2,1)S(1)} %bitcast.112, f32[]{:T(128)S(6)} %convert.61, f32[]{:T(128)S(6)} %convert.60, f32[]{:T(128)S(6)} %convert.59, f32[]{:T(128)S(6)} %convert.58, f32[]{:T(128)S(6)} %convert.57, f32[]{:T(128)S(6)} %convert.56, f32[]{:T(128)S(6)} %convert.55, ...), kind=kOutput, calls=%fused_computation.14 | convolution fusion | flops 159252480 | bytes 524412 | tf_op jit(solution)/shard_map/dot_general | solution.py:28
  45.8 0.9 broadcast_select_fusion
  46.8 44.3 %all-reduce.8.cloned.1.call-done = bf16[2,128,512]{1,0,2:T(2,128)(2,1)} async-done(((bf16[2,128,512]{1,0,2:T(2,128)(2,1)}), bf16[2,128,512]{1,0,2:T(2,128)(2,1)}) %all-reduce.8.cloned.1.call-update) | async-done | bytes 262160 | tf_op jit(solution)/shard_map/psum | solution.py:11
  91.0 1.2 pad.31
  92.3 149.7 %while.16 = (s32[]{:T(128)}, f32[256,256]{1,0:T(8,128)S(1)}, bf16[2,128,512]{1,0,2:T(2,128)(2,1)S(1)}, bf16[2,128,639]{1,0,2:T(2,128)(2,1)S(1)}, s32[128,128]{1,...) while((s32[]{:T(128)}, f32[256,256]{1,0:T(8,128)S(1)}, ...), condition=%wide.region_3.4_spmd.clone, body=%wide.region_1.3_spmd.clone.sunk | while | flops 1077157888 | bytes 58205932 | solution.py:82
  92.9 1.1 rev.37
  94.0 13.5 %fusion.165 = (f32[32,128,128]{1,0,2:T(8,128)S(1)}, f32[32,128,128]{1,0,2:T(8,128)S(1)}) fusion(f32[32,128]{1,0:T(8,128)S(1)} %fusion.164, bf16[2,128,639]{1,0,2:T(2,128)(2,1)S(1)} %get-tuple-element.323, bf16[2,32,512]{1,0,2:T(2,128)(2,1)S(1)} %rev.37), kind=kOutput, calls=%fused_computation.6.clone.1 | convolution fusion | flops 1074790400 | bytes 4603392 | tf_op jit(solution)/shard_map/while/body/eval_jaxpr/conv_general_dilated | solution.py:64
  107.5 2.4 pad_maximum_fusion.2
  109.9 5.2 %copy.31 = f32[32,128,256]{2,1,0:T(8,128)} copy(f32[32,128,256]{1,0,2:T(8,128)} %pad_maximum_fusion.2) | data formatting | bytes 8388608 | tf_op jit(solution)/shard_map/while
  115.1 2.8 %pad.36.clone.2 = f32[32,160,256]{2,1,0:T(8,128)S(1)} pad(f32[32,128,256]{2,1,0:T(8,128)} %copy.31, f32[]{:T(128)} %constant.243.clone.1..sunk), padding=0_0x0_32x0_0 | pad | bytes 9437188 | tf_op jit(solution)/shard_map/while/body/eval_jaxpr/jit(_pad)/pad | solution.py:34
  117.9 2.7 %slice.210 = f32[5088,256]{1,0:T(8,128)} slice(f32[5120,256]{1,0:T(8,128)S(1)} %bitcast.113), slice={[0:5088], [0:256]} | slice | bytes 10420224 | tf_op jit(solution)/shard_map/while/body/eval_jaxpr/slice | solution.py:35
  120.6 5.5 %reshape.274 = f32[32,159,256]{2,1,0:T(8,128)} reshape(f32[5088,256]{1,0:T(8,128)} %slice.210) | data formatting | bytes 10420224 | tf_op jit(solution)/shard_map/while/body/eval_jaxpr/reshape | solution.py:36
  126.1 2.8 %reduce_sum.28 = f32[159,256]{1,0:T(8,128)S(1)} reduce(f32[32,159,256]{2,1,0:T(8,128)} %reshape.274, f32[]{:T(128)} %constant.243.clone.1..sunk), dimensions={0}, to_apply=%region_2.2 | reduce | flops 1261824 | bytes 5372932 | tf_op jit(solution)/shard_map/while/body/eval_jaxpr/reduce_sum | solution.py:36
  130.1 1.1 rev.37
  131.2 13.5 %fusion.165 = (f32[32,128,128]{1,0,2:T(8,128)S(1)}, f32[32,128,128]{1,0,2:T(8,128)S(1)}) fusion(f32[32,128]{1,0:T(8,128)S(1)} %fusion.164, bf16[2,128,639]{1,0,2:T(2,128)(2,1)S(1)} %get-tuple-element.323, bf16[2,32,512]{1,0,2:T(2,128)(2,1)S(1)} %rev.37), kind=kOutput, calls=%fused_computation.6.clone.1 | convolution fusion | flops 1074790400 | bytes 4603392 | tf_op jit(solution)/shard_map/while/body/eval_jaxpr/conv_general_dilated | solution.py:64
  144.7 2.4 pad_maximum_fusion.2
  147.1 5.2 %copy.31 = f32[32,128,256]{2,1,0:T(8,128)} copy(f32[32,128,256]{1,0,2:T(8,128)} %pad_maximum_fusion.2) | data formatting | bytes 8388608 | tf_op jit(solution)/shard_map/while
  152.3 2.8 %pad.36.clone.2 = f32[32,160,256]{2,1,0:T(8,128)S(1)} pad(f32[32,128,256]{2,1,0:T(8,128)} %copy.31, f32[]{:T(128)} %constant.243.clone.1..sunk), padding=0_0x0_32x0_0 | pad | bytes 9437188 | tf_op jit(solution)/shard_map/while/body/eval_jaxpr/jit(_pad)/pad | solution.py:34
  155.1 2.7 %slice.210 = f32[5088,256]{1,0:T(8,128)} slice(f32[5120,256]{1,0:T(8,128)S(1)} %bitcast.113), slice={[0:5088], [0:256]} | slice | bytes 10420224 | tf_op jit(solution)/shard_map/while/body/eval_jaxpr/slice | solution.py:35
  157.8 5.5 %reshape.274 = f32[32,159,256]{2,1,0:T(8,128)} reshape(f32[5088,256]{1,0:T(8,128)} %slice.210) | data formatting | bytes 10420224 | tf_op jit(solution)/shard_map/while/body/eval_jaxpr/reshape | solution.py:36
  163.3 2.8 %reduce_sum.28 = f32[159,256]{1,0:T(8,128)S(1)} reduce(f32[32,159,256]{2,1,0:T(8,128)} %reshape.274, f32[]{:T(128)} %constant.243.clone.1..sunk), dimensions={0}, to_apply=%region_2.2 | reduce | flops 1261824 | bytes 5372932 | tf_op jit(solution)/shard_map/while/body/eval_jaxpr/reduce_sum | solution.py:36
  166.1 0.8 dynamic_update_slice.22
  167.4 1.1 rev.37
  168.6 13.5 %fusion.165 = (f32[32,128,128]{1,0,2:T(8,128)S(1)}, f32[32,128,128]{1,0,2:T(8,128)S(1)}) fusion(f32[32,128]{1,0:T(8,128)S(1)} %fusion.164, bf16[2,128,639]{1,0,2:T(2,128)(2,1)S(1)} %get-tuple-element.323, bf16[2,32,512]{1,0,2:T(2,128)(2,1)S(1)} %rev.37), kind=kOutput, calls=%fused_computation.6.clone.1 | convolution fusion | flops 1074790400 | bytes 4603392 | tf_op jit(solution)/shard_map/while/body/eval_jaxpr/conv_general_dilated | solution.py:64
  182.0 2.4 pad_maximum_fusion.2
  184.4 5.2 %copy.31 = f32[32,128,256]{2,1,0:T(8,128)} copy(f32[32,128,256]{1,0,2:T(8,128)} %pad_maximum_fusion.2) | data formatting | bytes 8388608 | tf_op jit(solution)/shard_map/while
  189.7 2.8 %pad.36.clone.2 = f32[32,160,256]{2,1,0:T(8,128)S(1)} pad(f32[32,128,256]{2,1,0:T(8,128)} %copy.31, f32[]{:T(128)} %constant.243.clone.1..sunk), padding=0_0x0_32x0_0 | pad | bytes 9437188 | tf_op jit(solution)/shard_map/while/body/eval_jaxpr/jit(_pad)/pad | solution.py:34
  192.4 2.7 %slice.210 = f32[5088,256]{1,0:T(8,128)} slice(f32[5120,256]{1,0:T(8,128)S(1)} %bitcast.113), slice={[0:5088], [0:256]} | slice | bytes 10420224 | tf_op jit(solution)/shard_map/while/body/eval_jaxpr/slice | solution.py:35
  195.1 5.5 %reshape.274 = f32[32,159,256]{2,1,0:T(8,128)} reshape(f32[5088,256]{1,0:T(8,128)} %slice.210) | data formatting | bytes 10420224 | tf_op jit(solution)/shard_map/while/body/eval_jaxpr/reshape | solution.py:36
  200.6 2.8 %reduce_sum.28 = f32[159,256]{1,0:T(8,128)S(1)} reduce(f32[32,159,256]{2,1,0:T(8,128)} %reshape.274, f32[]{:T(128)} %constant.243.clone.1..sunk), dimensions={0}, to_apply=%region_2.2 | reduce | flops 1261824 | bytes 5372932 | tf_op jit(solution)/shard_map/while/body/eval_jaxpr/reduce_sum | solution.py:36
  203.5 0.9 dynamic_update_slice.22
  204.8 1.1 rev.37
  206.0 13.5 %fusion.165 = (f32[32,128,128]{1,0,2:T(8,128)S(1)}, f32[32,128,128]{1,0,2:T(8,128)S(1)}) fusion(f32[32,128]{1,0:T(8,128)S(1)} %fusion.164, bf16[2,128,639]{1,0,2:T(2,128)(2,1)S(1)} %get-tuple-element.323, bf16[2,32,512]{1,0,2:T(2,128)(2,1)S(1)} %rev.37), kind=kOutput, calls=%fused_computation.6.clone.1 | convolution fusion | flops 1074790400 | bytes 4603392 | tf_op jit(solution)/shard_map/while/body/eval_jaxpr/conv_general_dilated | solution.py:64
  219.5 2.4 pad_maximum_fusion.2
  221.8 5.2 %copy.31 = f32[32,128,256]{2,1,0:T(8,128)} copy(f32[32,128,256]{1,0,2:T(8,128)} %pad_maximum_fusion.2) | data formatting | bytes 8388608 | tf_op jit(solution)/shard_map/while
  227.1 2.8 %pad.36.clone.2 = f32[32,160,256]{2,1,0:T(8,128)S(1)} pad(f32[32,128,256]{2,1,0:T(8,128)} %copy.31, f32[]{:T(128)} %constant.243.clone.1..sunk), padding=0_0x0_32x0_0 | pad | bytes 9437188 | tf_op jit(solution)/shard_map/while/body/eval_jaxpr/jit(_pad)/pad | solution.py:34
  229.9 2.7 %slice.210 = f32[5088,256]{1,0:T(8,128)} slice(f32[5120,256]{1,0:T(8,128)S(1)} %bitcast.113), slice={[0:5088], [0:256]} | slice | bytes 10420224 | tf_op jit(solution)/shard_map/while/body/eval_jaxpr/slice | solution.py:35
  232.5 5.5 %reshape.274 = f32[32,159,256]{2,1,0:T(8,128)} reshape(f32[5088,256]{1,0:T(8,128)} %slice.210) | data formatting | bytes 10420224 | tf_op jit(solution)/shard_map/while/body/eval_jaxpr/reshape | solution.py:36
  238.0 2.8 %reduce_sum.28 = f32[159,256]{1,0:T(8,128)S(1)} reduce(f32[32,159,256]{2,1,0:T(8,128)} %reshape.274, f32[]{:T(128)} %constant.243.clone.1..sunk), dimensions={0}, to_apply=%region_2.2 | reduce | flops 1261824 | bytes 5372932 | tf_op jit(solution)/shard_map/while/body/eval_jaxpr/reduce_sum | solution.py:36
  240.9 1.0 dynamic_update_slice.22
  242.7 0.8 select_bitcast_fusion
  243.5 4.6 %all-to-all-start = ((f32[9,32,128]{2,0,1:T(8,128)}), f32[9,32,128]{2,0,1:T(8,128)S(1)}, u32[]{:S(2)}, u32[]{:S(2)}) async-start(f32[9,32,128]{2,0,1:T(8,128)} %select_bitcast_fusion), calls=%async_computation | async-start | bytes 524288 | tf_op jit(solution)/shard_map/all_to_all | solution.py:104
  249.1 9.3 %all-to-all-done = f32[9,32,128]{2,0,1:T(8,128)S(1)} async-done(((f32[9,32,128]{2,0,1:T(8,128)}), f32[9,32,128]{2,0,1:T(8,128)S(1)}, u32[]{:S(2)}, u32[]{:S(2)}) %all-to-all-start) | async-done | bytes 147488 | tf_op jit(solution)/shard_map/all_to_all | solution.py:104
  258.5 0.9 fusion.8
  (60 shorter events, 7.7 us)
Async XLA Ops:
  6.5 35.1 %copy-start = (bf16[2,128,512]{2,1,0:T(8,128)(2,1)S(1)}, bf16[2,128,512]{2,1,0:T(8,128)(2,1)}, u32[]{:S(2)}) copy-start(bf16[2,128,512]{2,1,0:T(8,128)(2,1)} %param.6) | copy-start | bytes 786436
  10.9 232.6 %all-to-all-start.1 = ((f32[9,32,1]{0,2,1:T(1,128)}), f32[9,32,1]{0,2,1:T(1,128)S(1)}, u32[]{:S(2)}, u32[]{:S(2)}) async-start(f32[9,32,1]{0,2,1:T(1,128)} %bitcast.44), calls=%async_computation.1 | async-start | bytes 32768 | tf_op jit(solution)/shard_map/all_to_all | solution.py:105
  18.2 72.9 %all-reduce.8.cloned.1.call-start = ((), (), s32[]{:S(2)}) async-start(), calls=%async_computation.2 | async-start | bytes 524288 | tf_op jit(solution)/shard_map/psum | solution.py:11
  41.6 5.1 %copy-start.1 = (s32[128,128]{1,0:T(8,128)S(1)}, s32[128,128]{1,0:T(8,128)}, u32[]{:S(2)}) copy-start(s32[128,128]{1,0:T(8,128)} %param.8) | copy-start | bytes 196612
  243.5 15.0 %all-to-all-start = ((f32[9,32,128]{2,0,1:T(8,128)}), f32[9,32,128]{2,0,1:T(8,128)S(1)}, u32[]{:S(2)}, u32[]{:S(2)}) async-start(f32[9,32,128]{2,0,1:T(8,128)} %select_bitcast_fusion), calls=%async_computation | async-start | bytes 524288 | tf_op jit(solution)/shard_map/all_to_all | solution.py:104
Sparse Core Ops, SparseCore 0:
  46.8 44.1 all-reduce.7
where the time goes:
time: 268 us; the launch traced here: 266 us
  local copies, waits for them, and re-layouts  83.4 us (31%)
  matrix products  59 us (22%)
  waiting for transfers between devices  53.6 us (20%)
  between operations  33.2 us (12%)
  other arithmetic  24.6 us (9%)
  starting transfers between devices  11.9 us (4%)
    conv_general_dilated x4, matrix products, one_turn(): lax.conv_general_dilated(padded, rows, (1,), 'VALID', dimension_numbers=(...  53.9 us
    psum x1, waiting for transfers between devices, broadcast(): return lax.psum(block, axis)  44.3 us
    reshape x5, local copies, waits for them, and re-layouts, skew_sum(): return flat.reshape(rows, width + rows - 1, depth).sum(axis=0)  22.3 us
    while x4, local copies, waits for them, and re-layouts  21 us
    reduce_sum x5, other arithmetic, skew_sum(): return flat.reshape(rows, width + rows - 1, depth).sum(axis=0)  11.3 us
    pad x4, local copies, waits for them, and re-layouts, skew_sum(): padded = jnp.pad(block, ((0, 0), (0, rows), (0, 0)))  11.2 us
    slice x5, local copies, waits for them, and re-layouts, skew_sum(): padded.reshape(rows * (width + rows), depth)[:rows * (width + rows - 1)]  10.7 us
    concatenate x4, other arithmetic, one_turn(): jnp.concatenate([values - upper_part, upper_part], axis=2)  9.47 us
  transfers between devices with their start and end apart: 3, of which 2 were waited for; matrix products, arithmetic and copies ran while one was open for 61% of the time, Pallas kernels for 0%

commit v1 on v0

v1 whole, which is shorter than its diff:
```python
import functools

import jax
import jax.numpy as jnp
import ml_dtypes
import numpy as np
from jax import lax
from jax.experimental import pallas as pl
from jax.experimental.pallas import tpu as pltpu
from jax.sharding import PartitionSpec as P

MAXLAG = 64
LAGS = 2 * MAXLAG
BF16, F32 = jnp.bfloat16, jnp.float32
NT = (((1,), (1,)), ((), ()))
NN = (((1,), (0,)), ((), ()))
VMEM_BYTES = 56 * 2**20


def dot(a, b, dims=NN):
    return lax.dot_general(a, b, dims, preferred_element_type=F32)


def exact_dot(a, b):
    return lax.dot_general(a, b, NN, precision=lax.Precision.HIGHEST, preferred_element_type=F32)


def forward_table(length):
    period = length + MAXLAG
    angle = 2 * np.pi / period * (np.arange(period // 2)[:, None] + 0.5) * np.arange(length)[None, :]
    table = np.concatenate([np.cos(angle), -np.sin(angle)], 0)
    high = table.astype(ml_dtypes.bfloat16)
    low = (table - high.astype(np.float64)).astype(ml_dtypes.bfloat16)
    return np.concatenate([high, low], 1)


def inverse_table(length, group, slot, per_tile):
    period = length + MAXLAG
    groups = period // 2 // group
    lag = np.arange(LAGS) - MAXLAG
    table = np.zeros((group, slot, LAGS))
    for g in range(groups):
        angle = 2 * np.pi / period * (g * group + np.arange(group)[:, None] + 0.5) * lag[None, :]
        table[:, 2 * g] = 2 / period * np.cos(angle)
        table[:, 2 * g + 1] = -2 / period * np.sin(angle)
    return table.reshape(group * slot, LAGS).astype(np.float32)


def fir_kernel(half, taps, out):
    length = out.shape[0]
    spread = jnp.broadcast_to(taps[...], (length, length))
    rolled = pltpu.roll(spread, length - half, 1, stride=1, stride_axis=0)
    distance = lax.broadcasted_iota(jnp.int32, (length, length), 1) - lax.broadcasted_iota(
        jnp.int32, (length, length), 0
    )
    out[...] = jnp.where(jnp.abs(distance) <= half, rolled, 0.0).astype(out.dtype)


def fir_matrix(fir_taps, length):
    taps = jnp.pad(fir_taps.astype(F32)[None, :], ((0, 0), (0, length - fir_taps.shape[0])))
    return pl.pallas_call(
        functools.partial(fir_kernel, fir_taps.shape[0] // 2),
        out_shape=jax.ShapeDtypeStruct((length, length), fir_taps.dtype),
        in_specs=[pl.BlockSpec(memory_space=pltpu.VMEM)],
        out_specs=pl.BlockSpec(memory_space=pltpu.VMEM),
        name="fir_matrix",
    )(taps)


def transform(records, matrix, table, width, residues):
    filtered = dot(records, matrix).astype(BF16)
    segs = records.shape[0] // width
    rows = []
    for first in range(0, width, residues):
        rows.append(
            jnp.concatenate(
                [filtered[s * width + first : s * width + first + residues] for s in range(segs)], 0
            )
        )
    lanes = segs * residues
    batch = max(1, 256 // lanes)
    results = []
    for start in range(0, len(rows), batch):
        some = jnp.concatenate(rows[start : start + batch], 0)
        spectra = dot(table, jnp.concatenate([some, some], 1), NT).astype(BF16)
        for index in range(len(rows[start : start + batch])):
            results.append(spectra[:, index * lanes : (index + 1) * lanes])
    return results


def load_block(mine, mate, held, sems):
    rows = mine.shape[0]
    copies = [
        pltpu.make_async_copy(mine, held.at[pl.ds(0, rows)], sems.at[0]),
        pltpu.make_async_copy(mate, held.at[pl.ds(rows, rows)], sems.at[1]),
    ]
    for copy in copies:
        copy.start()
    return copies


def early_kernel(blocks, width, residues, matrix, table, *refs):
    sources, out, held, sems = refs[: 2 * blocks], refs[2 * blocks], refs[2 * blocks + 1], refs[2 * blocks + 2]
    copies = [
        load_block(sources[2 * k], sources[2 * k + 1], held.at[k], sems.at[k]) for k in range(blocks)
    ]
    per_block = width // residues
    for k in range(blocks):
        for copy in copies[k]:
            copy.wait()
        for index, rows in enumerate(transform(held[k], matrix[...], table[...], width, residues)):
            out[k * per_block + index] = rows


def late_kernel(
    width, residues, segs, length, src_count,
    scalars, matrix, table, inverse, ones_zeros, row_bins, early, mine, mate,
    out, held, spectra, edges, shifted, parts, sems, early_sems,
):
    src, shift = scalars[0], scalars[1]
    per_block = width // residues
    rows_q = spectra.shape[0] - 2
    freqs = (length + MAXLAG) // 2
    lanes = segs * residues
    group = 256 // rows_q
    groups = freqs // group
    last = src_count - 1
    loads = load_block(mine, mate, held, sems)
    moves = []
    for k in range(last):
        moves.append(
            pltpu.make_async_copy(
                early.at[pl.ds(k * per_block, per_block)],
                spectra.at[pl.ds(1 + per_block * (src ^ k), per_block), pl.ds(0, 2 * freqs)],
                early_sems.at[k],
            )
        )
        moves[-1].start()
    pad = jnp.zeros((2 * freqs + 16, lanes), BF16)
    spectra[0] = pad
    spectra[rows_q + 1] = pad
    one = jnp.ones((16, lanes), BF16)
    for q in range(rows_q):
        spectra[1 + q, 2 * freqs : 2 * freqs + 16] = one

    jitter = ones_zeros[...]
    blocks, block_lanes = jitter.shape
    edges[...] = jnp.zeros_like(edges)
    per_row = block_lanes // residues
    source_lane = lax.broadcasted_iota(jnp.int32, (block_lanes, lanes), 0)
    target_lane = lax.broadcasted_iota(jnp.int32, (block_lanes, lanes), 1)
    for index in range(per_row):
        pick = (source_lane == target_lane % residues + index * residues).astype(F32)
        spread = exact_dot(jitter, pick)
        for b in range(blocks):
            row = 8 + b * per_row + index
            edges[row : row + 1, :] = spread[b : b + 1, :]
    jitter_rows = edges[8 : 8 + rows_q, :]
    pairs = jnp.concatenate([edges[7:31, :], edges[8:32, :]], 1)
    pairs = jnp.concatenate([pairs, jnp.zeros((104, 2 * lanes), F32)], 0)
    jitter_columns = jnp.concatenate(
        [pairs[:, 128 * i : 128 * (i + 1)].T for i in range(2 * lanes // 128)], 0
    )

    row_lane = lax.broadcasted_iota(jnp.int32, (2 * lanes, lanes), 0)
    col_lane = lax.broadcasted_iota(jnp.int32, (2 * lanes, lanes), 1)
    same_seg = (row_lane % lanes) // residues == col_lane // residues
    place = (row_lane // lanes) * residues + row_lane % residues - col_lane % residues - shift
    here = jnp.where(same_seg & (place == 0), F32(1), F32(0))
    after = jnp.where(same_seg & (place == 1), F32(1), F32(0))
    here_bf = here.astype(BF16)
    difference = here - after

    for copy in loads:
        copy.wait()
    for index, rows in enumerate(transform(held[...], matrix[...], table[...], width, residues)):
        spectra[1 + per_block * (src ^ last) + index, 0 : 2 * freqs] = rows
    for move in moves:
        move.wait()

    for p in range(rows_q + 1):
        mix = after + difference * jitter_columns[:, p : p + 1]
        mapping = jnp.concatenate([here_bf, mix.astype(BF16)], 1)
        both = jnp.concatenate([spectra[p], spectra[p + 1]], 1)
        moved = dot(both, mapping).astype(BF16)
        shifted[p, 0 : 2 * freqs + 16] = moved
        shifted[p, 2 * freqs + 16 : 3 * freqs + 16] = -moved[0:freqs]

    upper = jitter_rows.astype(BF16)
    lower = (1.0 - jitter_rows).astype(BF16)
    freq_row = lax.broadcasted_iota(jnp.int32, (group, 256), 0)
    freq_lane = lax.broadcasted_iota(jnp.int32, (group, 256), 1)
    diagonal = freq_row == freq_lane % group
    slot_lane = lax.broadcasted_iota(jnp.int32, (8, 256), 1) // group

    def gather_bins(block, p, low, high):
        kept = jnp.where(diagonal, block, 0.0)
        total = kept[0:8]
        for i in range(1, group // 8):
            total = total + kept[8 * i : 8 * i + 8]
        amount = (256 - group * p) % 256
        if amount:
            total = pltpu.roll(total, amount, 1)
        if p == 0:
            return low + total, high
        if p == rows_q:
            return low, high + total
        first = slot_lane < rows_q - p
        return low + jnp.where(first, total, 0.0), high + jnp.where(first, 0.0, total)

    zero = jnp.zeros((8, 256), F32)
    parts[...] = jnp.zeros_like(parts)

    def one_group(g, carry):
        first = pl.multiple_of(g * group, group)
        real = pl.ds(first, group)
        imag = pl.ds(first + freqs, group)
        minus = pl.ds(first + 2 * freqs + 16, group)
        left = []
        for q in range(rows_q):
            re, im = spectra[1 + q, real], spectra[1 + q, imag]
            lo, up = lower[q : q + 1], upper[q : q + 1]
            left.append(jnp.concatenate([re * lo, re * up, im * lo, im * up], 1))
        right = []
        for p in range(rows_q + 1):
            re, im, neg = shifted[p, real], shifted[p, imag], shifted[p, minus]
            right.append(jnp.concatenate([re, im], 1))
            right.append(jnp.concatenate([im, neg], 1))
        product = dot(jnp.concatenate(right, 0), jnp.concatenate(left, 0), NT)
        sums = [zero] * 4
        for p in range(rows_q + 1):
            for part in range(2):
                start = (2 * p + part) * group
                sums[2 * part], sums[2 * part + 1] = gather_bins(
                    product[start : start + group], p, sums[2 * part], sums[2 * part + 1]
                )
        for part in range(2):
            for wrap in range(2):
                parts[wrap, pl.ds(2 * g + part, 1), :] = jnp.sum(sums[2 * part + wrap], 0, keepdims=True)
        return carry

    lax.fori_loop(0, groups, one_group, 0)

    count_left = []
    for q in range(rows_q):
        row = jnp.concatenate([lower[q : q + 1], upper[q : q + 1]], 1)
        count_left.append(jnp.broadcast_to(row, (group, 2 * lanes)))
    ones_rows = [shifted[p, 2 * freqs : 2 * freqs + 16] for p in range(rows_q + 1)]
    if group > 16:
        ones_rows = [jnp.concatenate([rows] * (group // 16), 0) for rows in ones_rows]
    counted = dot(jnp.concatenate(ones_rows, 0), jnp.concatenate(count_left, 0), NT)
    count_low, count_high = zero, zero
    for p in range(rows_q + 1):
        count_low, count_high = gather_bins(
            counted[p * group : (p + 1) * group], p, count_low, count_high
        )
    counts = jnp.concatenate(
        [jnp.sum(count_low, 0, keepdims=True), jnp.sum(count_high, 0, keepdims=True)], 1
    )

    used = parts.shape[1]
    per_tile = 128 // used
    freq_of_row = lax.broadcasted_iota(jnp.int32, (256, 128), 0) % group
    tile_slot = lax.broadcasted_iota(jnp.int32, (256, 128), 1) // used
    lagged = []
    for wrap in range(2):
        stacked = jnp.concatenate([parts[wrap]] * per_tile, 0)
        turned = jnp.concatenate([stacked[:, 0:128].T, stacked[:, 128:256].T], 0)
        tiles = [
            jnp.where(freq_of_row == tile_slot + per_tile * i, turned, 0.0)
            for i in range(group // per_tile)
        ]
        lagged.append(exact_dot(jnp.concatenate(tiles, 1), inverse[...]))
    lagged = jnp.concatenate(lagged, 0)

    bins = row_bins[...]
    owned = bins.shape[0]
    lane = lax.broadcasted_iota(jnp.int32, (owned, 512), 1)
    lane_bin = (lane // 256 + 1) * rows_q - 1 - lane % 256 // group
    picked = jnp.concatenate([bins] * 4, 1) == lane_bin
    total = exact_dot(jnp.where(picked, F32(1), F32(0)), lagged)
    count = jnp.sum(jnp.where(picked & (lane % group == 0), counts, 0.0), 1, keepdims=True) / segs
    out[...] = total * lax.rsqrt(jnp.maximum(count, 1.0) * (segs * length))


def partners(axis, step):
    return [(index, index ^ step) for index in range(lax.axis_size(axis))]


def on_device(traces, fir_taps, pair_bins, bin_order):
    seg_local, width, length = traces.shape
    src_count, rcv_count, seg_count = (lax.axis_size(axis) for axis in ("src", "rcv", "seg"))
    segs = seg_local * seg_count
    channels = width * src_count
    owners = src_count * rcv_count * seg_count
    residues = owners
    rows_q = channels // residues
    lanes = segs * residues
    period = length + MAXLAG
    group = 256 // rows_q
    owned = bin_order.shape[0] // owners
    src, rcv = lax.axis_index("src"), lax.axis_index("rcv")

    mine = traces.reshape(seg_local * width, length)
    received = [mine] + [lax.ppermute(mine, "src", partners("src", k)) for k in range(1, src_count)]
    receivers = pair_bins.shape[1]
    jitter = pair_bins[width - 1 : width, :] - (
        rcv * receivers + jnp.arange(receivers, dtype=jnp.int32)[None, :]
    )
    slots = jnp.arange(rcv_count, dtype=jnp.int32)[:, None]
    jitter = jnp.where((slots == rcv) & (src == src_count - 1), jitter, 0).astype(F32)
    for axis, count in (("rcv", rcv_count), ("src", src_count)):
        step = 1
        while step < count:
            jitter = jitter + lax.ppermute(jitter, axis, partners(axis, step))
            step *= 2

    mates = [lax.ppermute(block, "seg", partners("seg", 1)) for block in received]
    matrix = fir_matrix(fir_taps, length)
    table = jnp.asarray(forward_table(length))
    used = 1
    while used < period // group:
        used *= 2
    inverse = jnp.asarray(inverse_table(length, group, used, 128 // used))
    rank = (src * rcv_count + rcv) * seg_count + lax.axis_index("seg")
    own_bins = lax.dynamic_slice_in_dim(bin_order, rank * owned, owned, 0)
    row_bins = jnp.broadcast_to((own_bins // residues)[:, None], (owned, 128))
    scalars = jnp.stack([src, own_bins[0] % residues]).astype(jnp.int32)

    vmem = pl.BlockSpec(memory_space=pltpu.VMEM)
    smem = pl.BlockSpec(memory_space=pltpu.SMEM)
    hbm = pl.BlockSpec(memory_space=pl.ANY)
    last = src_count - 1
    per_block = width // residues
    early = pl.pallas_call(
        functools.partial(early_kernel, last, width, residues),
        out_shape=jax.ShapeDtypeStruct((last * per_block, period, lanes), BF16),
        in_specs=[vmem, vmem] + [hbm] * (2 * last),
        out_specs=vmem,
        scratch_shapes=[
            pltpu.VMEM((last, segs * width, length), BF16),
            pltpu.SemaphoreType.DMA((last, 2)),
        ],
        compiler_params=pltpu.CompilerParams(vmem_limit_bytes=VMEM_BYTES),
        name="early_spectra",
    )(matrix, table, *[a for k in range(last) for a in (received[k], mates[k])])
    return pl.pallas_call(
        functools.partial(late_kernel, width, residues, segs, length, src_count),
        out_shape=jax.ShapeDtypeStruct((owned, LAGS), F32),
        in_specs=[smem] + [vmem] * 5 + [hbm] * 3,
        out_specs=vmem,
        scratch_shapes=[
            pltpu.VMEM((segs * width, length), BF16),
            pltpu.VMEM((rows_q + 2, period + 16, lanes), BF16),
            pltpu.VMEM((32, lanes), F32),
            pltpu.VMEM((rows_q + 1, period + 16 + period // 2, 2 * lanes), BF16),
            pltpu.VMEM((2, used, 256), F32),
            pltpu.SemaphoreType.DMA((2,)),
            pltpu.SemaphoreType.DMA((last,)),
        ],
        compiler_params=pltpu.CompilerParams(vmem_limit_bytes=VMEM_BYTES),
        name="bin_stacks",
    )(scalars, matrix, table, inverse, jitter, row_bins, early, received[last], mates[last])


def solution(mesh):
    return jax.shard_map(
        on_device,
        mesh=mesh,
        in_specs=(P("seg", "src", None), P(), P("src", "rcv"), P()),
        out_specs=P(("src", "rcv", "seg"), None),
        check_vma=False,
    )
```

time: 268 us -> 53.5 us (0.20)
  local copies, waits for them, and re-layouts: 83.4 us -> 2.22 us
  matrix products: 59 us -> 0 us
  waiting for transfers between devices: 53.6 us -> 9.39 us
  between operations: 33.2 us -> 0.22 us
  Pallas kernels: 0 us -> 25.4 us
  other arithmetic: 24.6 us -> 4.09 us
    conv_general_dilated x4 -> x0, matrix products: 53.9 us -> none  [one_turn(): lax.conv_general_dilated(padded, rows, (1,), 'VALID', dimension_numbers=(...]
    psum x1 -> x0, waiting for transfers between devices: 44.3 us -> none  [broadcast(): return lax.psum(block, axis)]
    pallas_call x0 -> x3, Pallas kernels: none -> 25.4 us  [the longest x1 16.4 us: on_device(): pl.pallas_call(functools.partial(late_kernel, width, residues, segs, leng...]
    reshape x9 -> x0, local copies, waits for them, and re-layouts: 23.4 us -> none  [the longest x5 22.3 us: skew_sum(): return flat.reshape(rows, width + rows - 1, depth).sum(axis=0)]
    while x4 -> x0, local copies, waits for them, and re-layouts: 21 us -> none
    slice x9 -> x0, local copies, waits for them, and re-layouts: 14.6 us -> none  [the longest x5 10.7 us: skew_sum(): padded.reshape(rows * (width + rows), depth)[:rows * (width + rows - 1)]]
    pad x5 -> x0, local copies, waits for them, and re-layouts: 12.3 us -> none  [the longest x4 11.2 us: skew_sum(): padded = jnp.pad(block, ((0, 0), (0, rows), (0, 0)))]
    all_to_all x2 -> x0, starting transfers between devices: 11.9 us -> none  [the longest x1 7.3 us: on_device(): lax.all_to_all(outgoing_counts, ('src', 'rcv', 'seg'), split_axis=1, conc...]
  transfers between devices with their start and end apart: 3 -> 11, of which waited for: 2 -> 3; matrix products, arithmetic and copies ran while one was open for 61% -> 6% of each run, Pallas kernels for 0% -> 17%
where the time goes in v1:
time: 53.5 us; the launch traced here: 53.2 us
  Pallas kernels  25.4 us (47%)
  starting transfers between devices  11.9 us (22%)
  waiting for transfers between devices  9.39 us (18%)
  other arithmetic  4.09 us (8%)
  local copies, waits for them, and re-layouts  2.22 us (4%)
    pallas_call x1, Pallas kernels, on_device(): pl.pallas_call(functools.partial(late_kernel, width, residues, segs, leng...  16.4 us
    ppermute x4, starting transfers between devices, on_device(): jitter = jitter + lax.ppermute(jitter, axis, partners(axis, step))  7.87 us
    ppermute x3, waiting for transfers between devices, on_device(): lax.ppermute(mine, 'src', partners('src', k))  7.41 us
    pallas_call x1, Pallas kernels, on_device(): pl.pallas_call(functools.partial(early_kernel, last, width, residues), ou...  7.37 us
    ppermute x3, starting transfers between devices, on_device(): lax.ppermute(mine, 'src', partners('src', k))  3.49 us
    ppermute x4, waiting for transfers between devices, on_device(): jitter = jitter + lax.ppermute(jitter, axis, partners(axis, step))  1.97 us
    pallas_call x1, Pallas kernels, fir_matrix(): pl.pallas_call(functools.partial(fir_kernel, fir_taps.shape[0] // 2), out...  1.59 us
    unnamed x14, local copies, waits for them, and re-layouts  1.51 us
  transfers between devices with their start and end apart: 11, of which 3 were waited for; matrix products, arithmetic and copies ran while one was open for 6% of the time, Pallas kernels for 17%

profile of v1, /device:TPU:0, one launch (start us, length us, event | category | flops | bytes accessed | tf_op | source)
XLA Modules:
  0.0 53.2 jit_solution(101667897373243999)
XLA Ops:
  0.0 0.7 %subtract_bitcast_fusion = s32[128]{0:T(128)S(1)} fusion(s32[128,128]{1,0:T(8,128)} %param.8, s32[]{:T(128)S(6)} %mul.15), kind=kLoop, calls=%fused_computation.8 | loop fusion | flops 256 | bytes 1028 | tf_op jit(solution)/shard_map/jit(_where)/broadcast_in_dim | solution.py:311
  0.7 0.1 select_convert_fusion
  0.8 3.0 %collective-permute-start = (f32[4,128]{1,0:T(4,128)S(1)}, f32[4,128]{1,0:T(4,128)S(1)}, u32[]{:S(2)}, u32[]{:S(2)}) collective-permute-start(f32[4,128]{1,0:T(4,128)S(1)} %select_convert_fusion), channel_id=1, source_target_pairs={{0,2},{2,0},{4,6},{6,4},{1,3},{3,1},{5,7},{7,5},{8,10},{10,8},{12,... | collective-permute-start | bytes 6152 | tf_op jit(solution)/shard_map/ppermute | solution.py:315
  3.8 1.5 %collective-permute-start.5 = (bf16[256,512]{1,0:T(8,128)(2,1)}, bf16[256,512]{1,0:T(8,128)(2,1)S(1)}, u32[]{:S(2)}, u32[]{:S(2)}) collective-permute-start(bf16[256,512]{1,0:T(8,128)(2,1)} %bitcast.8), channel_id=1, source_target_pairs={{0,8},{8,0},{16,24},{24,16},{1,9},{9,1},{17,25},{25,17},{2,10},{10... | collective-permute-start | bytes 786440 | tf_op jit(solution)/shard_map/ppermute | solution.py:305
  5.3 1.5 %collective-permute-start.7 = (bf16[256,512]{1,0:T(8,128)(2,1)}, bf16[256,512]{1,0:T(8,128)(2,1)S(1)}, u32[]{:S(2)}, u32[]{:S(2)}) collective-permute-start(bf16[256,512]{1,0:T(8,128)(2,1)} %bitcast.9), channel_id=1, source_target_pairs={{0,16},{8,24},{16,0},{24,8},{1,17},{9,25},{17,1},{25,9},{2,18},{10... | collective-permute-start | bytes 786440 | tf_op jit(solution)/shard_map/ppermute | solution.py:305
  6.8 0.0 collective-permute-start.4
  6.8 0.5 collective-permute-start.9
  7.3 0.0 collective-permute-done
  7.3 0.1 fusion
  7.4 2.6 %collective-permute-start.1 = (f32[4,128]{1,0:T(4,128)S(1)}, f32[4,128]{1,0:T(4,128)S(1)}, u32[]{:S(2)}, u32[]{:S(2)}) collective-permute-start(f32[4,128]{1,0:T(4,128)S(1)} %fusion), channel_id=1, source_target_pairs={{0,4},{2,6},{4,0},{6,2},{1,5},{3,7},{5,1},{7,3},{8,12},{10,14},{12... | collective-permute-start | bytes 6152 | tf_op jit(solution)/shard_map/ppermute | solution.py:315
  10.0 1.2 %pad_convert_fusion.taps = f32[1,512]{1,0:T(1,128)} fusion(bf16[1,31]{1,0:T(2,128)(2,1)} %bitcast.16), kind=kLoop, calls=%fused_computation.1 | loop fusion | flops 512 | bytes 2110 | tf_op jit(solution)/shard_map/jit(_pad)/pad | solution.py:60
  11.2 2.0 %collective-permute-done.5.refs_2_ = bf16[256,512]{1,0:T(8,128)(2,1)S(1)} collective-permute-done((bf16[256,512]{1,0:T(8,128)(2,1)}, bf16[256,512]{1,0:T(8,128)(2,1)S(1)}, u32[]{:S(2)}, u32[]{:S(2)}) %collective-permute-start.5) | collective-permute-done | bytes 262176 | tf_op jit(solution)/shard_map/ppermute | solution.py:305
  13.2 0.0 copy-start.1
  13.2 0.0 collective-permute-start.6
  13.2 5.4 %collective-permute-done.7.refs_4_ = bf16[256,512]{1,0:T(8,128)(2,1)S(1)} collective-permute-done((bf16[256,512]{1,0:T(8,128)(2,1)}, bf16[256,512]{1,0:T(8,128)(2,1)S(1)}, u32[]{:S(2)}, u32[]{:S(2)}) %collective-permute-start.7) | collective-permute-done | bytes 262176 | tf_op jit(solution)/shard_map/ppermute | solution.py:305
  18.6 0.0 copy-start.2
  18.6 0.0 collective-permute-start.8
  18.6 0.0 collective-permute-done.9.mine
  18.6 0.0 copy-start
  18.6 0.5 collective-permute-start.10
  19.1 0.0 collective-permute-done.1
  19.1 0.1 fusion.1
  19.2 0.7 %collective-permute-start.2 = (f32[4,128]{1,0:T(4,128)S(1)}, f32[4,128]{1,0:T(4,128)S(1)}, u32[]{:S(2)}, u32[]{:S(2)}) collective-permute-start(f32[4,128]{1,0:T(4,128)S(1)} %fusion.1), channel_id=1, source_target_pairs={{0,8},{8,0},{16,24},{24,16},{1,9},{9,1},{17,25},{25,17},{2,10},{10... | collective-permute-start | bytes 6152 | tf_op jit(solution)/shard_map/ppermute | solution.py:315
  19.9 0.8 %and_select_fusion = (s32[32]{0:T(128)S(1)}, s32[32]{0:T(128)S(1)}) fusion(s32[1024]{0:T(1024)} %param.9, s32[]{:T(128)S(6)} %select_n.19), kind=kLoop, calls=%fused_computation.2 | loop fusion | flops 480 | bytes 388 | tf_op jit(solution)/shard_map/jit(floor_divide)/jit(_where)/select_n | solution.py:327
  20.8 2.0 %collective-permute-done.2 = f32[4,128]{1,0:T(4,128)S(1)} collective-permute-done((f32[4,128]{1,0:T(4,128)S(1)}, f32[4,128]{1,0:T(4,128)S(1)}, u32[]{:S(2)}, u32[]{:S(2)}) %collective-permute-start.2) | collective-permute-done | bytes 2080 | tf_op jit(solution)/shard_map/ppermute | solution.py:315
  22.8 1.5 %collective-permute-start.3 = (f32[4,128]{1,0:T(4,128)S(1)}, f32[4,128]{1,0:T(4,128)S(1)}, u32[]{:S(2)}, u32[]{:S(2)}) collective-permute-start(f32[4,128]{1,0:T(4,128)S(1)} %add.50), channel_id=1, source_target_pairs={{0,16},{8,24},{16,0},{24,8},{1,17},{9,25},{17,1},{25,9},{2,18},{10... | collective-permute-start | bytes 6152 | tf_op jit(solution)/shard_map/ppermute | solution.py:315
  24.3 0.6 %pad_add_fusion.scalars = s32[2]{0:T(128)} fusion(s32[1]{0:T(128)} %bitcast.2, s32[1]{0:T(128)} %bitcast), kind=kLoop, calls=%fused_computation.7 | loop fusion | flops 2 | bytes 16 | tf_op jit(solution)/shard_map/stack | solution.py:328
  24.9 1.6 %fir_matrix.1.matrix = bf16[512,512]{1,0:T(8,128)(2,1)} custom-call(f32[1,512]{1,0:T(1,128)} %pad_convert_fusion.taps), custom_call_target="tpu_custom_call" | custom-call | tf_op jit(solution)/shard_map/fir_matrix/pallas_call | solution.py:61
  26.5 0.0 collective-permute-done.3
  26.5 0.6 %add.51.ones_zeros = f32[4,128]{1,0:T(4,128)} add(f32[4,128]{1,0:T(4,128)S(1)} %add.50, f32[4,128]{1,0:T(4,128)S(1)} %collective-permute-done.3) | non-fusion elementwise | flops 512 | bytes 6144 | tf_op jit(solution)/shard_map/add | solution.py:315
  27.1 0.0 collective-permute-done.4.refs_1_
  27.1 0.0 copy-start.3
  27.1 0.0 collective-permute-done.6.refs_3_
  27.1 0.0 copy-start.4
  27.1 0.0 collective-permute-done.8.refs_5_
  27.1 0.0 copy-done.1
  27.1 0.0 copy-done.2
  27.1 0.6 %copy-done.3 = bf16[256,512]{1,0:T(8,128)(2,1)} copy-done((bf16[256,512]{1,0:T(8,128)(2,1)}, bf16[256,512]{1,0:T(8,128)(2,1)S(1)}, u32[]{:S(2)}) %copy-start.3) | copy-done | bytes 262168
  27.8 0.1 copy-done.4
  27.9 0.0 copy-start.6
  27.9 0.7 %copy-done.6 = bf16[256,512]{1,0:T(8,128)(2,1)} copy-done((bf16[256,512]{1,0:T(8,128)(2,1)}, bf16[256,512]{1,0:T(8,128)(2,1)S(1)}, u32[]{:S(2)}) %copy-start.6) | copy-done | bytes 262168
  28.6 7.4 %early_spectra.1.early = bf16[12,576,128]{2,1,0:T(8,128)(2,1)} custom-call(bf16[512,512]{1,0:T(8,128)(2,1)} %fir_matrix.1.matrix, bf16[576,1024]{1,0:T(8,128)(2,1)} %constant.55.clone.table, bf16[256,512]{1,0:T(8,128)(2,1)} %bitcast.12, bf16[256,512]{1,0:T(8,128)(2,1)} %copy-done.3, bf16[256,512]{1,0:T(8,128)(2,1)} %copy-done.1, bf16[256,512]{1,0:T(8,128)(2,1)} %copy-done.4, ...), custom_call_target="tpu_custom_call" | custom-call | tf_op jit(solution)/shard_map/early_spectra/pallas_call | solution.py:335
  36.0 0.0 copy-done
  36.0 0.0 collective-permute-done.10.mate
  36.0 0.0 copy-start.5
  36.0 0.7 %broadcast_in_dim.39.row_bins = s32[32,128]{1,0:T(8,128)} broadcast(s32[32]{0:T(128)S(1)} %get-tuple-element.5), dimensions={0} | broadcast | bytes 16512 | tf_op jit(solution)/shard_map/broadcast_in_dim | solution.py:327
  36.7 0.0 copy-done.5
  36.7 16.4 %bin_stacks.1 = f32[32,128]{1,0:T(8,128)} custom-call(s32[2]{0:T(128)} %pad_add_fusion.scalars, bf16[512,512]{1,0:T(8,128)(2,1)} %fir_matrix.1.matrix, bf16[576,1024]{1,0:T(8,128)(2,1)} %constant.55.clone.table, f32[1024,128]{1,0:T(8,128)} %constant.56.clone.inverse, f32[4,128]{1,0:T(4,128)} %add.51.ones_zeros, s32[32,128]{1,0:T(8,128)} %broadcast_in_dim.39.row_bins, ...), custom_call_target="tpu_custom_call" | custom-call | tf_op jit(solution)/shard_map/bin_stacks/pallas_call | solution.py:347
  (2 shorter events, 0.0 us)
Async XLA Ops:
  0.8 6.5 %collective-permute-start = (f32[4,128]{1,0:T(4,128)S(1)}, f32[4,128]{1,0:T(4,128)S(1)}, u32[]{:S(2)}, u32[]{:S(2)}) collective-permute-start(f32[4,128]{1,0:T(4,128)S(1)} %select_convert_fusion), channel_id=1, source_target_pairs={{0,2},{2,0},{4,6},{6,4},{1,3},{3,1},{5,7},{7,5},{8,10},{10,8},{12,... | collective-permute-start | bytes 6152 | tf_op jit(solution)/shard_map/ppermute | solution.py:315
  3.8 9.4 %collective-permute-start.5 = (bf16[256,512]{1,0:T(8,128)(2,1)}, bf16[256,512]{1,0:T(8,128)(2,1)S(1)}, u32[]{:S(2)}, u32[]{:S(2)}) collective-permute-start(bf16[256,512]{1,0:T(8,128)(2,1)} %bitcast.8), channel_id=1, source_target_pairs={{0,8},{8,0},{16,24},{24,16},{1,9},{9,1},{17,25},{25,17},{2,10},{10... | collective-permute-start | bytes 786440 | tf_op jit(solution)/shard_map/ppermute | solution.py:305
  5.3 13.3 %collective-permute-start.7 = (bf16[256,512]{1,0:T(8,128)(2,1)}, bf16[256,512]{1,0:T(8,128)(2,1)S(1)}, u32[]{:S(2)}, u32[]{:S(2)}) collective-permute-start(bf16[256,512]{1,0:T(8,128)(2,1)} %bitcast.9), channel_id=1, source_target_pairs={{0,16},{8,24},{16,0},{24,8},{1,17},{9,25},{17,1},{25,9},{2,18},{10... | collective-permute-start | bytes 786440 | tf_op jit(solution)/shard_map/ppermute | solution.py:305
  6.8 20.3 %collective-permute-start.4 = (bf16[256,512]{1,0:T(8,128)(2,1)}, bf16[256,512]{1,0:T(8,128)(2,1)S(1)}, u32[]{:S(2)}, u32[]{:S(2)}) collective-permute-start(bf16[256,512]{1,0:T(8,128)(2,1)} %bitcast.10), channel_id=1, source_target_pairs={{0,1},{1,0},{2,3},{3,2},{4,5},{5,4},{6,7},{7,6},{8,9},{9,8},{10,11... | collective-permute-start | bytes 786440 | tf_op jit(solution)/shard_map/ppermute | solution.py:318
  6.8 11.8 %collective-permute-start.9 = (bf16[256,512]{1,0:T(8,128)(2,1)}, bf16[256,512]{1,0:T(8,128)(2,1)S(1)}, u32[]{:S(2)}, u32[]{:S(2)}) collective-permute-start(bf16[256,512]{1,0:T(8,128)(2,1)} %bitcast.11), channel_id=1, source_target_pairs={{0,24},{8,16},{16,8},{24,0},{1,25},{9,17},{17,9},{25,1},{2,26},{10... | collective-permute-start | bytes 786440 | tf_op jit(solution)/shard_map/ppermute | solution.py:305
  7.4 11.8 %collective-permute-start.1 = (f32[4,128]{1,0:T(4,128)S(1)}, f32[4,128]{1,0:T(4,128)S(1)}, u32[]{:S(2)}, u32[]{:S(2)}) collective-permute-start(f32[4,128]{1,0:T(4,128)S(1)} %fusion), channel_id=1, source_target_pairs={{0,4},{2,6},{4,0},{6,2},{1,5},{3,7},{5,1},{7,3},{8,12},{10,14},{12... | collective-permute-start | bytes 6152 | tf_op jit(solution)/shard_map/ppermute | solution.py:315
  13.2 13.9 %copy-start.1 = (bf16[256,512]{1,0:T(8,128)(2,1)}, bf16[256,512]{1,0:T(8,128)(2,1)S(1)}, u32[]{:S(2)}) copy-start(bf16[256,512]{1,0:T(8,128)(2,1)S(1)} %collective-permute-done.5.refs_2_) | copy-start | bytes 786436
  13.2 13.8 %collective-permute-start.6 = (bf16[256,512]{1,0:T(8,128)(2,1)S(1)}, bf16[256,512]{1,0:T(8,128)(2,1)S(1)}, u32[]{:S(2)}, u32[]{:S(2)}) collective-permute-start(bf16[256,512]{1,0:T(8,128)(2,1)S(1)} %collective-permute-done.5.refs_2_), channel_id=1, source_target_pairs={{0,1},{1,0},{2,3},{3,2},{4,5},{5,4},{6,7},{7,6},{8,9},{9,8},{10,11... | collective-permute-start | bytes 786440 | tf_op jit(solution)/shard_map/ppermute | solution.py:318
  18.6 8.5 %copy-start.2 = (bf16[256,512]{1,0:T(8,128)(2,1)}, bf16[256,512]{1,0:T(8,128)(2,1)S(1)}, u32[]{:S(2)}) copy-start(bf16[256,512]{1,0:T(8,128)(2,1)S(1)} %collective-permute-done.7.refs_4_) | copy-start | bytes 786436
  18.6 8.5 %collective-permute-start.8 = (bf16[256,512]{1,0:T(8,128)(2,1)S(1)}, bf16[256,512]{1,0:T(8,128)(2,1)S(1)}, u32[]{:S(2)}, u32[]{:S(2)}) collective-permute-start(bf16[256,512]{1,0:T(8,128)(2,1)S(1)} %collective-permute-done.7.refs_4_), channel_id=1, source_target_pairs={{0,1},{1,0},{2,3},{3,2},{4,5},{5,4},{6,7},{7,6},{8,9},{9,8},{10,11... | collective-permute-start | bytes 786440 | tf_op jit(solution)/shard_map/ppermute | solution.py:318
  18.6 17.4 %copy-start = (bf16[256,512]{1,0:T(8,128)(2,1)}, bf16[256,512]{1,0:T(8,128)(2,1)S(1)}, u32[]{:S(2)}) copy-start(bf16[256,512]{1,0:T(8,128)(2,1)S(1)} %collective-permute-done.9.mine) | copy-start | bytes 786436
  18.6 17.4 %collective-permute-start.10 = (bf16[256,512]{1,0:T(8,128)(2,1)S(1)}, bf16[256,512]{1,0:T(8,128)(2,1)S(1)}, u32[]{:S(2)}, u32[]{:S(2)}) collective-permute-start(bf16[256,512]{1,0:T(8,128)(2,1)S(1)} %collective-permute-done.9.mine), channel_id=1, source_target_pairs={{0,1},{1,0},{2,3},{3,2},{4,5},{5,4},{6,7},{7,6},{8,9},{9,8},{10,11... | collective-permute-start | bytes 786440 | tf_op jit(solution)/shard_map/ppermute | solution.py:318
  19.2 3.6 %collective-permute-start.2 = (f32[4,128]{1,0:T(4,128)S(1)}, f32[4,128]{1,0:T(4,128)S(1)}, u32[]{:S(2)}, u32[]{:S(2)}) collective-permute-start(f32[4,128]{1,0:T(4,128)S(1)} %fusion.1), channel_id=1, source_target_pairs={{0,8},{8,0},{16,24},{24,16},{1,9},{9,1},{17,25},{25,17},{2,10},{10... | collective-permute-start | bytes 6152 | tf_op jit(solution)/shard_map/ppermute | solution.py:315
  22.8 3.7 %collective-permute-start.3 = (f32[4,128]{1,0:T(4,128)S(1)}, f32[4,128]{1,0:T(4,128)S(1)}, u32[]{:S(2)}, u32[]{:S(2)}) collective-permute-start(f32[4,128]{1,0:T(4,128)S(1)} %add.50), channel_id=1, source_target_pairs={{0,16},{8,24},{16,0},{24,8},{1,17},{9,25},{17,1},{25,9},{2,18},{10... | collective-permute-start | bytes 6152 | tf_op jit(solution)/shard_map/ppermute | solution.py:315
  27.1 0.7 %copy-start.3 = (bf16[256,512]{1,0:T(8,128)(2,1)}, bf16[256,512]{1,0:T(8,128)(2,1)S(1)}, u32[]{:S(2)}) copy-start(bf16[256,512]{1,0:T(8,128)(2,1)S(1)} %collective-permute-done.4.refs_1_) | copy-start | bytes 786436
  27.1 0.8 %copy-start.4 = (bf16[256,512]{1,0:T(8,128)(2,1)}, bf16[256,512]{1,0:T(8,128)(2,1)S(1)}, u32[]{:S(2)}) copy-start(bf16[256,512]{1,0:T(8,128)(2,1)S(1)} %collective-permute-done.6.refs_3_) | copy-start | bytes 786436
  27.9 0.7 %copy-start.6 = (bf16[256,512]{1,0:T(8,128)(2,1)}, bf16[256,512]{1,0:T(8,128)(2,1)S(1)}, u32[]{:S(2)}) copy-start(bf16[256,512]{1,0:T(8,128)(2,1)S(1)} %collective-permute-done.8.refs_5_) | copy-start | bytes 786436
  36.0 0.7 %copy-start.5 = (bf16[256,512]{1,0:T(8,128)(2,1)}, bf16[256,512]{1,0:T(8,128)(2,1)S(1)}, u32[]{:S(2)}) copy-start(bf16[256,512]{1,0:T(8,128)(2,1)S(1)} %collective-permute-done.10.mate) | copy-start | bytes 786436

commit v2 on v0

v2 whole, which is shorter than its diff:
```python
import functools

import jax
import jax.numpy as jnp
import ml_dtypes
import numpy as np
from jax import lax
from jax.experimental import pallas as pl
from jax.experimental.pallas import tpu as pltpu
from jax.sharding import PartitionSpec as P

MAXLAG = 64
LAGS = 2 * MAXLAG
BF16, F32 = jnp.bfloat16, jnp.float32
NT = (((1,), (1,)), ((), ()))
NN = (((1,), (0,)), ((), ()))
UNROLL = 36


def dot(a, b, dims=NN):
    return lax.dot_general(a, b, dims, preferred_element_type=F32)


def exact_dot(a, b):
    return lax.dot_general(a, b, NN, precision=lax.Precision.HIGHEST, preferred_element_type=F32)


def frequencies(length):
    period = length + MAXLAG
    return 2 * np.pi / period * (np.arange(period // 2) + 0.5)


def angle_parts(length, group):
    width = length + MAXLAG
    first, time = frequencies(length)[:group], np.arange(length)
    stride = frequencies(length)[::group] - first[0]
    column = np.repeat(frequencies(length).reshape(-1, 1, group), 2, 1).reshape(-1)
    parts = []
    for angle in (stride[:, None] * time, first[:, None] * time):
        parts += [np.pad(table, ((0, 0), (0, MAXLAG))) for table in (np.cos(angle), np.sin(angle))]
    for lag in (np.arange(-MAXLAG, MAXLAG, 8), np.arange(8)):
        angle = lag[:, None] * column
        parts += [np.cos(angle), np.sin(angle)]
    assert all(part.shape[1] == width for part in parts)
    return np.concatenate([np.pad(p, ((0, -p.shape[0] % 8), (0, 0))) for p in parts]).astype(np.float32)


def store_halves(ref, rows, value, times):
    width = value.shape[1]
    high = value.astype(BF16)
    low = (value - high.astype(F32)).astype(BF16)
    order = (high, low) if times == 2 else (high, high, low)
    ref[rows] = jnp.concatenate(order, 1)


def prepare_kernel(half, group, taps, parts, matrix_t, table, inverse):
    length = matrix_t.shape[0]
    row = jnp.concatenate([taps[...].astype(F32), jnp.zeros((1, length - taps.shape[1]), F32)], 1)
    spread = jnp.broadcast_to(row, (length, length))
    rolled = pltpu.roll(spread, length - half, 1, stride=1, stride_axis=0).T
    distance = lax.broadcasted_iota(jnp.int32, (length, length), 1) - lax.broadcasted_iota(
        jnp.int32, (length, length), 0
    )
    matrix_t[...] = jnp.where(jnp.abs(distance) <= half, rolled, 0.0).astype(matrix_t.dtype)

    groups = (length + MAXLAG) // 2 // group
    padded = groups + -groups % 8
    cos_first, sin_first = (parts[2 * padded + i * group : 2 * padded + (i + 1) * group, 0:length] for i in range(2))
    for g in range(groups):
        cos_step, sin_step = parts[g : g + 1, 0:length], parts[padded + g : padded + g + 1, 0:length]
        real = cos_first * cos_step - sin_first * sin_step
        imag = -(sin_first * cos_step + cos_first * sin_step)
        store_halves(table, pl.ds(2 * g * group, 2 * group), jnp.concatenate([real, imag], 0), 2)

    base = 2 * padded + 2 * group
    steps = LAGS // 8
    cos_first, sin_first = (parts[base + 2 * steps + 8 * i : base + 2 * steps + 8 * (i + 1), :] for i in range(2))
    lane = lax.broadcasted_iota(jnp.int32, (8, length + MAXLAG), 1)
    is_real = (lane & group) == 0
    scale = F32(2.0 / (length + MAXLAG))
    for step in range(steps):
        cos_step = parts[base + step : base + step + 1, :] * scale
        sin_step = parts[base + steps + step : base + steps + step + 1, :] * scale
        cosine = cos_first * cos_step - sin_first * sin_step
        sine = sin_first * cos_step + cos_first * sin_step
        store_halves(inverse, pl.ds(8 * step, 8), jnp.where(is_real, cosine, -sine), 3)
        store_halves(inverse, pl.ds(LAGS + 8 * step, 8), jnp.where(is_real, sine, cosine), 3)


def transform(records, matrix_t, table, width, residues):
    segs = records.shape[0] // width
    rows = [
        records[s * width + first : s * width + first + residues]
        for first in range(0, width, residues)
        for s in range(segs)
    ]
    filtered = dot(matrix_t, jnp.concatenate(rows, 0), NT).astype(BF16)
    return dot(table, jnp.concatenate([filtered, filtered], 0)).astype(BF16)


def block_kernel(width, residues, matrix_t, table, mine, mate, out):
    records = jnp.concatenate([mine[...], mate[...]], 0)
    spectra = transform(records, matrix_t[...], table[...], width, residues)
    lanes = out.shape[2]
    for index in range(out.shape[0]):
        out[index] = spectra[:, index * lanes : (index + 1) * lanes]


def bin_lanes(product, first_row, rows_per, group, rows_q):
    width = 256 // rows_q
    per = 128 // width
    lane = lax.broadcasted_iota(jnp.int32, (group, 128), 1)

    def tile(p, half):
        start = p * rows_per + first_row
        return product[start : start + group, 128 * half : 128 * half + 128]

    total = [tile(2 * per, 0), tile(per, 0) + tile(2 * per, 1), tile(0, 0) + tile(per, 1), tile(0, 1)]
    for p in range(1, per):
        kept = width * (per - p)
        moved = [
            pltpu.roll(part, kept, 1)
            for part in (tile(per + p, 0), tile(p, 0) + tile(per + p, 1), tile(p, 1))
        ]
        inside = lane < kept
        total[0] = total[0] + jnp.where(inside, 0.0, moved[0])
        total[1] = total[1] + jnp.where(inside, moved[0], moved[1])
        total[2] = total[2] + jnp.where(inside, moved[1], moved[2])
        total[3] = total[3] + jnp.where(inside, moved[2], 0.0)
    place = lax.broadcasted_iota(jnp.int32, (group, 128), 0)
    diagonal = place == (lane & (group - 1))
    return jnp.concatenate([jnp.where(diagonal, part, 0.0) for part in total], 1)


def late_kernel(
    width, residues, segs, length, src_count,
    jitter_ref, arrived, bin_order, matrix_t, table, inverse, *refs,
):
    early, refs = refs[: src_count - 1], refs[src_count - 1 :]
    mine, mate, out, spectra, edges, shifted, binned = refs
    src = lax.axis_index("src")
    owned = out.shape[0]
    rank = lax.axis_index(("src", "rcv", "seg"))
    per_line = 128 // owned
    order = pltpu.roll(bin_order[pl.ds(rank // per_line, 1), :], 128 - owned * (rank % per_line), 1)
    square = (owned, 128)
    same = lax.broadcasted_iota(jnp.int32, square, 0) == lax.broadcasted_iota(jnp.int32, square, 1)
    bins = jnp.sum(jnp.where(same, jnp.broadcast_to(order, square), 0), 1, keepdims=True)
    shift = bins[0:1, 0:1] & (residues - 1)
    per_block = width // residues
    rows_q = spectra.shape[0] - 2
    height = length + MAXLAG
    lanes = segs * residues
    step = 256 // rows_q
    group = step // 2
    last = src_count - 1
    pad = jnp.zeros((height + 16, lanes), BF16)
    spectra[0] = pad
    spectra[rows_q + 1] = pad
    one = jnp.ones((16, lanes), BF16)
    for q in range(rows_q):
        spectra[1 + q, height : height + 16] = one

    jitter = jitter_ref[...] + arrived[...]
    blocks, block_lanes = jitter.shape
    edges[...] = jnp.zeros_like(edges)
    source_lane = lax.broadcasted_iota(jnp.int32, (block_lanes, lanes), 0)
    target_lane = lax.broadcasted_iota(jnp.int32, (block_lanes, lanes), 1) & (residues - 1)
    per_row = block_lanes // residues
    for index in range(per_row):
        pick = jnp.where(source_lane == target_lane + index * residues, F32(1), F32(0))
        spread = dot(jitter.astype(BF16), pick.astype(BF16))
        for b in range(blocks):
            row = 8 + b * per_row + index
            edges[row : row + 1, :] = spread[b : b + 1, :]
    jitter_rows = edges[8 : 8 + rows_q, :]
    pairs = jnp.concatenate([edges[7:31, :], edges[8:32, :]], 1)
    pairs = jnp.concatenate([pairs, jnp.zeros((104, 2 * lanes), F32)], 0)
    jitter_columns = jnp.concatenate(
        [pairs[:, 128 * i : 128 * (i + 1)].T for i in range(2 * lanes // 128)], 0
    )

    row_lane = lax.broadcasted_iota(jnp.int32, (2 * lanes, lanes), 0)
    col_lane = lax.broadcasted_iota(jnp.int32, (2 * lanes, lanes), 1)
    bits = residues.bit_length() - 1
    same_seg = ((row_lane & (lanes - 1)) >> bits) == (col_lane >> bits)
    inside = (row_lane & (residues - 1)) - (col_lane & (residues - 1)) - shift
    place = inside + jnp.where(row_lane >= lanes, residues, 0)
    here = jnp.where(same_seg & (place == 0), F32(1), F32(0))
    after = jnp.where(same_seg & (place == 1), F32(1), F32(0))
    here_bf = here.astype(BF16)
    difference = here - after

    records = jnp.concatenate([mine[...], mate[...]], 0)
    fresh = transform(records, matrix_t[...], table[...], width, residues)
    for index in range(per_block):
        spectra[1 + per_block * (src ^ last) + index, 0:height] = fresh[:, index * lanes : (index + 1) * lanes]
    for k in range(last):
        for index in range(per_block):
            spectra[1 + per_block * (src ^ k) + index, 0:height] = early[k][index]

    for p in range(rows_q + 1):
        mix = after + difference * jitter_columns[:, p : p + 1]
        mapping = jnp.concatenate([here_bf, mix.astype(BF16)], 1)
        both = jnp.concatenate([spectra[p], spectra[p + 1]], 1)
        shifted[p] = dot(both, mapping).astype(BF16)

    upper = jitter_rows.astype(BF16)
    lower = (1.0 - jitter_rows).astype(BF16)

    def one_group(g, carry):
        rows = pl.ds(pl.multiple_of(g * step, step), step)
        left = []
        for q in range(rows_q):
            values = spectra[1 + q, rows]
            left.append(jnp.concatenate([values * lower[q : q + 1], values * upper[q : q + 1]], 1))
        right = [shifted[p, rows] for p in range(rows_q + 1)]
        product = dot(jnp.concatenate(right, 0), jnp.concatenate(left, 0), NT)
        binned[rows] = jnp.concatenate(
            [bin_lanes(product, part * group, step, group, rows_q) for part in range(2)], 0
        )
        return carry

    lax.fori_loop(0, height // step, one_group, 0, unroll=UNROLL)

    count_left = []
    for q in range(rows_q):
        row = jnp.concatenate([lower[q : q + 1], upper[q : q + 1]], 1)
        count_left.append(jnp.broadcast_to(row, (step, 2 * lanes)))
    ones_rows = [shifted[p, height : height + 16] for p in range(rows_q + 1)]
    counted = dot(jnp.concatenate(ones_rows, 0), jnp.concatenate(count_left, 0), NT)
    if group > 8:
        counted = jnp.concatenate([counted[16 * p : 16 * p + 16] for p in range(rows_q + 1)], 0)
    counts = jnp.sum(bin_lanes(counted, 0, 16, group, rows_q), 0, keepdims=True)

    values = binned[...]
    high = values.astype(BF16)
    low = (values - high.astype(F32)).astype(BF16)
    lagged = dot(inverse[...], jnp.concatenate([high, low, high], 0))
    lane = lax.broadcasted_iota(jnp.int32, (LAGS, 512), 1)
    lagged = jnp.where((lane & group) == 0, lagged[0:LAGS], lagged[LAGS:])
    high = lagged.astype(BF16)
    low = (lagged - high.astype(F32)).astype(BF16)

    lane = lax.broadcasted_iota(jnp.int32, (owned, 512), 1)
    lane_bin = 2 * rows_q - 1 - (lane >> (step.bit_length() - 1))
    picked = (bins >> (residues.bit_length() - 1)) == lane_bin
    weights = jnp.where(picked, F32(1), F32(0))
    total = dot(
        jnp.concatenate([weights, weights], 1).astype(BF16), jnp.concatenate([high, low], 1), NT
    )
    count = jnp.sum(jnp.where((lane & (step - 1)) == 0, weights * counts, 0.0), 1, keepdims=True) / segs
    out[...] = total * lax.rsqrt(jnp.maximum(count, 1.0) * (segs * length))


def cost(microseconds):
    return pl.CostEstimate(
        flops=int(microseconds * 1e9), bytes_accessed=int(microseconds * 3e6), transcendentals=0
    )


def partners(axis, step):
    return [(index, index ^ step) for index in range(lax.axis_size(axis))]


def on_device(traces, fir_taps, pair_bins, bin_order):
    seg_local, width, length = traces.shape
    src_count, rcv_count, seg_count = (lax.axis_size(axis) for axis in ("src", "rcv", "seg"))
    segs = seg_local * seg_count
    channels = width * src_count
    owners = src_count * rcv_count * seg_count
    residues = owners
    rows_q = channels // residues
    lanes = segs * residues
    period = length + MAXLAG
    owned = bin_order.shape[0] // owners

    mine = traces.reshape(seg_local * width, length)
    received = [mine] + [lax.ppermute(mine, "src", partners("src", k)) for k in range(1, src_count)]
    mates = [lax.ppermute(mine, "seg", partners("seg", 1))]

    src, rcv = lax.axis_index("src"), lax.axis_index("rcv")
    receivers = pair_bins.shape[1]
    jitter = pair_bins[width - 1 : width, :] - (
        rcv * receivers + jnp.arange(receivers, dtype=jnp.int32)[None, :]
    )
    slots = jnp.arange(rcv_count, dtype=jnp.int32)[:, None]
    jitter = jnp.where((slots == rcv) & (src == src_count - 1), jitter, 0).astype(F32)

    vmem = pl.BlockSpec(memory_space=pltpu.VMEM)
    last = src_count - 1
    per_block = width // residues
    params = pltpu.CompilerParams(vmem_limit_bytes=(20 if lanes <= 128 else 40) * 2**20)
    group = 128 // rows_q
    matrix_t, table, inverse = pl.pallas_call(
        functools.partial(prepare_kernel, fir_taps.shape[0] // 2, group),
        out_shape=[
            jax.ShapeDtypeStruct((length, length), BF16),
            jax.ShapeDtypeStruct((period, 2 * length), BF16),
            jax.ShapeDtypeStruct((2 * LAGS, 3 * period), BF16),
        ],
        in_specs=[vmem] * 2,
        out_specs=[vmem] * 3,
        compiler_params=params,
        cost_estimate=cost(0.01),
        name="prepare",
    )(fir_taps[None, :], jnp.asarray(angle_parts(length, group)))

    def block_spectra(k):
        return pl.pallas_call(
            functools.partial(block_kernel, width, residues),
            out_shape=jax.ShapeDtypeStruct((per_block, period, lanes), BF16),
            in_specs=[vmem] * 4,
            out_specs=vmem,
            compiler_params=params,
            cost_estimate=cost(0.01),
            name="block_spectra",
        )(matrix_t, table, received[k], mates[k])

    hops = [("rcv", 1 << bit) for bit in range((rcv_count - 1).bit_length())]
    hops += [("src", 1 << bit) for bit in range((src_count - 1).bit_length())]
    arrived = jnp.zeros_like(jitter)
    early = [block_spectra(0)]
    for turn, (axis, step) in enumerate(hops):
        if turn == len(hops) - 1:
            *received[1:], early[0], arrived = lax.optimization_barrier((*received[1:], early[0], arrived))
            mates += [lax.ppermute(block, "seg", partners("seg", 1)) for block in received[1:]]
        jitter = jitter + arrived
        arrived = lax.ppermute(jitter, axis, partners(axis, step))
    early += [block_spectra(k) for k in range(1, last)]
    return pl.pallas_call(
        functools.partial(late_kernel, width, residues, segs, length, src_count),
        out_shape=jax.ShapeDtypeStruct((owned, LAGS), F32),
        in_specs=[vmem] * (last + 8),
        out_specs=vmem,
        scratch_shapes=[
            pltpu.VMEM((rows_q + 2, period + 16, lanes), BF16),
            pltpu.VMEM((32, lanes), F32),
            pltpu.VMEM((rows_q + 1, period + 16, 2 * lanes), BF16),
            pltpu.VMEM((period, 512), F32),
        ],
        compiler_params=params,
        cost_estimate=cost(0.01),
        name="bin_stacks",
    )(jitter, arrived, bin_order.reshape(-1, 128), matrix_t, table, inverse, *early, received[last], mates[last])


def solution(mesh):
    return jax.shard_map(
        on_device,
        mesh=mesh,
        in_specs=(P("seg", "src", None), P(), P("src", "rcv"), P()),
        out_specs=P(("src", "rcv", "seg"), None),
        check_vma=False,
    )
```

time: 268 us -> 30.3 us (0.11)
  local copies, waits for them, and re-layouts: 83.4 us -> 2.59 us
  matrix products: 59 us -> 0 us
  waiting for transfers between devices: 53.6 us -> 3.46 us
  between operations: 33.2 us -> 0.11 us
  other arithmetic: 24.6 us -> 0.92 us
  Pallas kernels: 0 us -> 10.5 us
    conv_general_dilated x4 -> x0, matrix products: 53.9 us -> none  [one_turn(): lax.conv_general_dilated(padded, rows, (1,), 'VALID', dimension_numbers=(...]
    psum x1 -> x0, waiting for transfers between devices: 44.3 us -> none  [broadcast(): return lax.psum(block, axis)]
    reshape x9 -> x0, local copies, waits for them, and re-layouts: 23.4 us -> none  [the longest x5 22.3 us: skew_sum(): return flat.reshape(rows, width + rows - 1, depth).sum(axis=0)]
    while x4 -> x0, local copies, waits for them, and re-layouts: 21 us -> none
    slice x9 -> x0, local copies, waits for them, and re-layouts: 14.6 us -> none  [the longest x5 10.7 us: skew_sum(): padded.reshape(rows * (width + rows), depth)[:rows * (width + rows - 1)]]
    ppermute x0 -> x11, starting transfers between devices: none -> 12.5 us  [the longest x4 8.37 us: on_device(): arrived = lax.ppermute(jitter, axis, partners(axis, step))]
    pad x5 -> x0, local copies, waits for them, and re-layouts: 12.3 us -> none  [the longest x4 11.2 us: skew_sum(): padded = jnp.pad(block, ((0, 0), (0, rows), (0, 0)))]
    all_to_all x2 -> x0, starting transfers between devices: 11.9 us -> none  [the longest x1 7.3 us: on_device(): lax.all_to_all(outgoing_counts, ('src', 'rcv', 'seg'), split_axis=1, conc...]
  transfers between devices with their start and end apart: 3 -> 11, of which waited for: 2 -> 2; matrix products, arithmetic and copies ran while one was open for 61% -> 0% of each run, Pallas kernels for 0% -> 14%
where the time goes in v2:
time: 30.3 us; the launch traced here: 30.1 us
  starting transfers between devices  12.5 us (41%)
  Pallas kernels  10.5 us (35%)
  waiting for transfers between devices  3.46 us (11%)
  local copies, waits for them, and re-layouts  2.59 us (9%)
  other arithmetic  0.92 us (3%)
    ppermute x4, starting transfers between devices, on_device(): arrived = lax.ppermute(jitter, axis, partners(axis, step))  8.37 us
    pallas_call x1, Pallas kernels, on_device(): pl.pallas_call(functools.partial(late_kernel, width, residues, segs, leng...  6.34 us
    ppermute x3, starting transfers between devices, on_device(): lax.ppermute(mine, 'src', partners('src', k))  3.49 us
    pallas_call x3, Pallas kernels, block_spectra(): pl.pallas_call(functools.partial(block_kernel, width, residues), out_shap...  3.45 us
    ppermute x4, waiting for transfers between devices, on_device(): arrived = lax.ppermute(jitter, axis, partners(axis, step))  3.44 us
    unnamed x8, local copies, waits for them, and re-layouts  2.59 us
    broadcast_in_dim x1, other arithmetic, on_device(): jnp.where((slots == rcv) & (src == src_count - 1), jitter, 0).astype(F32)  0.69 us
    pallas_call x1, Pallas kernels, on_device(): pl.pallas_call(functools.partial(prepare_kernel, fir_taps.shape[0] // 2,...  0.67 us
  transfers between devices with their start and end apart: 11, of which 2 were waited for; matrix products, arithmetic and copies ran while one was open for 0% of the time, Pallas kernels for 14%

profile of v2, /device:TPU:0, one launch (start us, length us, event | category | flops | bytes accessed | tf_op | source)
XLA Modules:
  0.0 30.1 jit_solution(15532739756611121704)
XLA Ops:
  0.0 0.7 %subtract_bitcast_fusion = s32[128]{0:T(128)S(1)} fusion(s32[128,128]{1,0:T(8,128)} %param.7, s32[]{:T(128)S(6)} %mul.3), kind=kLoop, calls=%fused_computation.2 | loop fusion | flops 256 | bytes 1028 | tf_op jit(solution)/shard_map/jit(_where)/broadcast_in_dim | solution.py:288
  0.7 0.1 select_convert_fusion
  0.8 3.0 %collective-permute-start = (f32[4,128]{1,0:T(4,128)S(1)}, f32[4,128]{1,0:T(4,128)S(1)}, u32[]{:S(2)}, u32[]{:S(2)}) collective-permute-start(f32[4,128]{1,0:T(4,128)S(1)} %select_convert_fusion), channel_id=1, source_target_pairs={{0,2},{2,0},{4,6},{6,4},{1,3},{3,1},{5,7},{7,5},{8,10},{10,8},{12,... | collective-permute-start | bytes 6152 | tf_op jit(solution)/shard_map/ppermute | solution.py:329
  3.8 0.0 collective-permute-start.5
  3.8 2.4 %collective-permute-start.4 = (bf16[256,512]{1,0:T(8,128)(2,1)}, bf16[256,512]{1,0:T(8,128)(2,1)S(1)}, u32[]{:S(2)}, u32[]{:S(2)}) collective-permute-start(bf16[256,512]{1,0:T(8,128)(2,1)} %bitcast.6), channel_id=1, source_target_pairs={{0,24},{8,16},{16,8},{24,0},{1,25},{9,17},{17,9},{25,1},{2,26},{10... | collective-permute-start | bytes 786440 | tf_op jit(solution)/shard_map/ppermute | solution.py:279
  6.2 0.5 %collective-permute-start.3 = (bf16[256,512]{1,0:T(8,128)(2,1)}, bf16[256,512]{1,0:T(8,128)(2,1)S(1)}, u32[]{:S(2)}, u32[]{:S(2)}) collective-permute-start(bf16[256,512]{1,0:T(8,128)(2,1)} %bitcast.7), channel_id=1, source_target_pairs={{0,16},{8,24},{16,0},{24,8},{1,17},{9,25},{17,1},{25,9},{2,18},{10... | collective-permute-start | bytes 786440 | tf_op jit(solution)/shard_map/ppermute | solution.py:279
  6.8 0.5 %collective-permute-start.2 = (bf16[256,512]{1,0:T(8,128)(2,1)}, bf16[256,512]{1,0:T(8,128)(2,1)S(1)}, u32[]{:S(2)}, u32[]{:S(2)}) collective-permute-start(bf16[256,512]{1,0:T(8,128)(2,1)} %bitcast.8), channel_id=1, source_target_pairs={{0,8},{8,0},{16,24},{24,16},{1,9},{9,1},{17,25},{25,17},{2,10},{10... | collective-permute-start | bytes 786440 | tf_op jit(solution)/shard_map/ppermute | solution.py:279
  7.3 0.0 collective-permute-done
  7.3 0.1 fusion
  7.4 2.6 %collective-permute-start.1 = (f32[4,128]{1,0:T(4,128)S(1)}, f32[4,128]{1,0:T(4,128)S(1)}, u32[]{:S(2)}, u32[]{:S(2)}) collective-permute-start(f32[4,128]{1,0:T(4,128)S(1)} %fusion), channel_id=1, source_target_pairs={{0,4},{2,6},{4,0},{6,2},{1,5},{3,7},{5,1},{7,3},{8,12},{10,14},{12... | collective-permute-start | bytes 6152 | tf_op jit(solution)/shard_map/ppermute | solution.py:329
  10.0 1.9 %collective-permute-done.1 = f32[4,128]{1,0:T(4,128)S(1)} collective-permute-done((f32[4,128]{1,0:T(4,128)S(1)}, f32[4,128]{1,0:T(4,128)S(1)}, u32[]{:S(2)}, u32[]{:S(2)}) %collective-permute-start.1) | collective-permute-done | bytes 2080 | tf_op jit(solution)/shard_map/ppermute | solution.py:329
  11.9 0.1 fusion.1
  11.9 1.5 %collective-permute-start.6 = (f32[4,128]{1,0:T(4,128)S(1)}, f32[4,128]{1,0:T(4,128)S(1)}, u32[]{:S(2)}, u32[]{:S(2)}) collective-permute-start(f32[4,128]{1,0:T(4,128)S(1)} %fusion.1), channel_id=1, source_target_pairs={{0,8},{8,0},{16,24},{24,16},{1,9},{9,1},{17,25},{25,17},{2,10},{10... | collective-permute-start | bytes 6152 | tf_op jit(solution)/shard_map/ppermute | solution.py:329
  13.4 0.0 copy-start
  13.4 1.0 %copy-done = f32[144,576]{1,0:T(8,128)S(1)} copy-done((f32[144,576]{1,0:T(8,128)S(1)}, f32[144,576]{1,0:T(8,128)}, u32[]{:S(2)}) %copy-start) | copy-done | bytes 331800
  14.4 0.0 copy-start.3
  14.4 0.7 %copy-done.3 = bf16[31]{0:T(256)(128)(2,1)S(1)} copy-done((bf16[31]{0:T(256)(128)(2,1)S(1)}, bf16[31]{0:T(256)(128)(2,1)}, u32[]{:S(2)}) %copy-start.3) | copy-done | bytes 86
  15.1 0.7 %prepare.1 = (bf16[512,512]{1,0:T(8,128)(2,1)S(1)}, bf16[576,1024]{1,0:T(8,128)(2,1)S(1)}, bf16[256,1728]{1,0:T(8,128)(2,1)S(1)}) custom-call(bf16[1,31]{1,0:T(2,128)(2,1)S(1)} %bitcast.11, f32[144,576]{1,0:T(8,128)S(1)} %copy-done), custom_call_target="tpu_custom_call" | custom-call | flops 10000000 | bytes 30000 | tf_op jit(solution)/shard_map/prepare/pallas_call | solution.py:295
  15.7 0.0 collective-permute-done.5.mate
  15.7 0.0 copy-start.1
  15.8 0.9 %copy-done.1 = bf16[2,128,512]{2,1,0:T(8,128)(2,1)S(1)} copy-done((bf16[2,128,512]{2,1,0:T(8,128)(2,1)S(1)}, bf16[2,128,512]{2,1,0:T(8,128)(2,1)}, u32[]{:S(2)}) %copy-start.1) | copy-done | bytes 262168
  16.7 1.1 %block_spectra.3.refs_0_ = bf16[4,576,128]{2,1,0:T(8,128)(2,1)S(1)} custom-call(bf16[512,512]{1,0:T(8,128)(2,1)S(1)} %get-tuple-element.13.matrix_t, bf16[576,1024]{1,0:T(8,128)(2,1)S(1)} %get-tuple-element.14.table, bf16[256,512]{1,0:T(8,128)(2,1)S(1)} %bitcast.9, bf16[256,512]{1,0:T(8,128)(2,1)S(1)} %collective-permute-done.5.mate), custom_call_target="tpu_custom_call" | custom-call | flops 10000000 | bytes 30000 | tf_op jit(solution)/shard_map/block_spectra/pallas_call | solution.py:310
  17.9 1.5 %collective-permute-done.6 = f32[4,128]{1,0:T(4,128)S(1)} collective-permute-done((f32[4,128]{1,0:T(4,128)S(1)}, f32[4,128]{1,0:T(4,128)S(1)}, u32[]{:S(2)}, u32[]{:S(2)}) %collective-permute-start.6) | collective-permute-done | bytes 2080 | tf_op jit(solution)/shard_map/ppermute | solution.py:329
  19.4 0.0 collective-permute-done.4.refs_3_
  19.4 0.0 collective-permute-done.3.mine
  19.4 0.0 collective-permute-done.2.mine
  19.4 0.1 collective-permute-start.8
  19.5 0.5 %collective-permute-start.9 = (bf16[256,512]{1,0:T(8,128)(2,1)S(1)}, bf16[256,512]{1,0:T(8,128)(2,1)S(1)}, u32[]{:S(2)}, u32[]{:S(2)}) collective-permute-start(bf16[256,512]{1,0:T(8,128)(2,1)S(1)} %collective-permute-done.3.mine), channel_id=1, source_target_pairs={{0,1},{1,0},{2,3},{3,2},{4,5},{5,4},{6,7},{7,6},{8,9},{9,8},{10,11... | collective-permute-start | bytes 786440 | tf_op jit(solution)/shard_map/ppermute | solution.py:327
  20.0 0.1 collective-permute-start.10
  20.1 1.3 %collective-permute-start.7 = (f32[4,128]{1,0:T(4,128)S(1)}, f32[4,128]{1,0:T(4,128)S(1)}, u32[]{:S(2)}, u32[]{:S(2)}) collective-permute-start(f32[4,128]{1,0:T(4,128)S(1)} %add.27.jitter_ref), channel_id=1, source_target_pairs={{0,16},{8,24},{16,0},{24,8},{1,17},{9,25},{17,1},{25,9},{2,18},{10... | collective-permute-start | bytes 6152 | tf_op jit(solution)/shard_map/ppermute | solution.py:329
  21.3 0.0 collective-permute-done.8.mate
  21.3 1.2 %block_spectra.4.refs_1_ = bf16[4,576,128]{2,1,0:T(8,128)(2,1)S(1)} custom-call(bf16[512,512]{1,0:T(8,128)(2,1)S(1)} %get-tuple-element.13.matrix_t, bf16[576,1024]{1,0:T(8,128)(2,1)S(1)} %get-tuple-element.14.table, bf16[256,512]{1,0:T(8,128)(2,1)S(1)} %collective-permute-done.2.mine, bf16[256,512]{1,0:T(8,128)(2,1)S(1)} %collective-permute-done.8.mate), custom_call_target="tpu_custom_call" | custom-call | flops 10000000 | bytes 30000 | tf_op jit(solution)/shard_map/block_spectra/pallas_call | solution.py:310
  22.5 0.0 copy-start.2
  22.5 0.0 collective-permute-done.9.mate
  22.5 1.2 %block_spectra.5.refs_2_ = bf16[4,576,128]{2,1,0:T(8,128)(2,1)S(1)} custom-call(bf16[512,512]{1,0:T(8,128)(2,1)S(1)} %get-tuple-element.13.matrix_t, bf16[576,1024]{1,0:T(8,128)(2,1)S(1)} %get-tuple-element.14.table, bf16[256,512]{1,0:T(8,128)(2,1)S(1)} %collective-permute-done.3.mine, bf16[256,512]{1,0:T(8,128)(2,1)S(1)} %collective-permute-done.9.mate), custom_call_target="tpu_custom_call" | custom-call | flops 10000000 | bytes 30000 | tf_op jit(solution)/shard_map/block_spectra/pallas_call | solution.py:310
  23.7 0.0 collective-permute-done.7.arrived
  23.7 0.0 collective-permute-done.10.refs_4_
  23.7 0.0 copy-done.2
  23.7 6.3 %bin_stacks.1 = f32[32,128]{1,0:T(8,128)} custom-call(f32[4,128]{1,0:T(4,128)S(1)} %add.27.jitter_ref, f32[4,128]{1,0:T(4,128)S(1)} %collective-permute-done.7.arrived, s32[8,128]{1,0:T(8,128)S(1)} %bitcast.10, bf16[512,512]{1,0:T(8,128)(2,1)S(1)} %get-tuple-element.13.matrix_t, bf16[576,1024]{1,0:T(8,128)(2,1)S(1)} %get-tuple-element.14.table, ...), custom_call_target="tpu_custom_call" | custom-call | flops 10000000 | bytes 30000 | tf_op jit(solution)/shard_map/bin_stacks/pallas_call | solution.py:331
  (2 shorter events, 0.0 us)
Async XLA Ops:
  0.8 6.5 %collective-permute-start = (f32[4,128]{1,0:T(4,128)S(1)}, f32[4,128]{1,0:T(4,128)S(1)}, u32[]{:S(2)}, u32[]{:S(2)}) collective-permute-start(f32[4,128]{1,0:T(4,128)S(1)} %select_convert_fusion), channel_id=1, source_target_pairs={{0,2},{2,0},{4,6},{6,4},{1,3},{3,1},{5,7},{7,5},{8,10},{10,8},{12,... | collective-permute-start | bytes 6152 | tf_op jit(solution)/shard_map/ppermute | solution.py:329
  3.8 11.9 %collective-permute-start.5 = (bf16[256,512]{1,0:T(8,128)(2,1)}, bf16[256,512]{1,0:T(8,128)(2,1)S(1)}, u32[]{:S(2)}, u32[]{:S(2)}) collective-permute-start(bf16[256,512]{1,0:T(8,128)(2,1)} %bitcast.5), channel_id=1, source_target_pairs={{0,1},{1,0},{2,3},{3,2},{4,5},{5,4},{6,7},{7,6},{8,9},{9,8},{10,11... | collective-permute-start | bytes 786440 | tf_op jit(solution)/shard_map/ppermute | solution.py:280
  3.8 15.6 %collective-permute-start.4 = (bf16[256,512]{1,0:T(8,128)(2,1)}, bf16[256,512]{1,0:T(8,128)(2,1)S(1)}, u32[]{:S(2)}, u32[]{:S(2)}) collective-permute-start(bf16[256,512]{1,0:T(8,128)(2,1)} %bitcast.6), channel_id=1, source_target_pairs={{0,24},{8,16},{16,8},{24,0},{1,25},{9,17},{17,9},{25,1},{2,26},{10... | collective-permute-start | bytes 786440 | tf_op jit(solution)/shard_map/ppermute | solution.py:279
  6.2 13.1 %collective-permute-start.3 = (bf16[256,512]{1,0:T(8,128)(2,1)}, bf16[256,512]{1,0:T(8,128)(2,1)S(1)}, u32[]{:S(2)}, u32[]{:S(2)}) collective-permute-start(bf16[256,512]{1,0:T(8,128)(2,1)} %bitcast.7), channel_id=1, source_target_pairs={{0,16},{8,24},{16,0},{24,8},{1,17},{9,25},{17,1},{25,9},{2,18},{10... | collective-permute-start | bytes 786440 | tf_op jit(solution)/shard_map/ppermute | solution.py:279
  6.8 12.6 %collective-permute-start.2 = (bf16[256,512]{1,0:T(8,128)(2,1)}, bf16[256,512]{1,0:T(8,128)(2,1)S(1)}, u32[]{:S(2)}, u32[]{:S(2)}) collective-permute-start(bf16[256,512]{1,0:T(8,128)(2,1)} %bitcast.8), channel_id=1, source_target_pairs={{0,8},{8,0},{16,24},{24,16},{1,9},{9,1},{17,25},{25,17},{2,10},{10... | collective-permute-start | bytes 786440 | tf_op jit(solution)/shard_map/ppermute | solution.py:279
  7.4 4.5 %collective-permute-start.1 = (f32[4,128]{1,0:T(4,128)S(1)}, f32[4,128]{1,0:T(4,128)S(1)}, u32[]{:S(2)}, u32[]{:S(2)}) collective-permute-start(f32[4,128]{1,0:T(4,128)S(1)} %fusion), channel_id=1, source_target_pairs={{0,4},{2,6},{4,0},{6,2},{1,5},{3,7},{5,1},{7,3},{8,12},{10,14},{12... | collective-permute-start | bytes 6152 | tf_op jit(solution)/shard_map/ppermute | solution.py:329
  11.9 7.5 %collective-permute-start.6 = (f32[4,128]{1,0:T(4,128)S(1)}, f32[4,128]{1,0:T(4,128)S(1)}, u32[]{:S(2)}, u32[]{:S(2)}) collective-permute-start(f32[4,128]{1,0:T(4,128)S(1)} %fusion.1), channel_id=1, source_target_pairs={{0,8},{8,0},{16,24},{24,16},{1,9},{9,1},{17,25},{25,17},{2,10},{10... | collective-permute-start | bytes 6152 | tf_op jit(solution)/shard_map/ppermute | solution.py:329
  13.4 1.0 %copy-start = (f32[144,576]{1,0:T(8,128)S(1)}, f32[144,576]{1,0:T(8,128)}, u32[]{:S(2)}) copy-start(f32[144,576]{1,0:T(8,128)} %constant.17.clone.parts) | copy-start | bytes 995332
  14.4 0.7 %copy-start.3 = (bf16[31]{0:T(256)(128)(2,1)S(1)}, bf16[31]{0:T(256)(128)(2,1)}, u32[]{:S(2)}) copy-start(bf16[31]{0:T(256)(128)(2,1)} %param.6) | copy-start | bytes 190
  15.7 1.0 %copy-start.1 = (bf16[2,128,512]{2,1,0:T(8,128)(2,1)S(1)}, bf16[2,128,512]{2,1,0:T(8,128)(2,1)}, u32[]{:S(2)}) copy-start(bf16[2,128,512]{2,1,0:T(8,128)(2,1)} %param.5) | copy-start | bytes 786436
  19.4 1.9 %collective-permute-start.8 = (bf16[256,512]{1,0:T(8,128)(2,1)S(1)}, bf16[256,512]{1,0:T(8,128)(2,1)S(1)}, u32[]{:S(2)}, u32[]{:S(2)}) collective-permute-start(bf16[256,512]{1,0:T(8,128)(2,1)S(1)} %collective-permute-done.2.mine), channel_id=1, source_target_pairs={{0,1},{1,0},{2,3},{3,2},{4,5},{5,4},{6,7},{7,6},{8,9},{9,8},{10,11... | collective-permute-start | bytes 786440 | tf_op jit(solution)/shard_map/ppermute | solution.py:327
  19.5 3.0 %collective-permute-start.9 = (bf16[256,512]{1,0:T(8,128)(2,1)S(1)}, bf16[256,512]{1,0:T(8,128)(2,1)S(1)}, u32[]{:S(2)}, u32[]{:S(2)}) collective-permute-start(bf16[256,512]{1,0:T(8,128)(2,1)S(1)} %collective-permute-done.3.mine), channel_id=1, source_target_pairs={{0,1},{1,0},{2,3},{3,2},{4,5},{5,4},{6,7},{7,6},{8,9},{9,8},{10,11... | collective-permute-start | bytes 786440 | tf_op jit(solution)/shard_map/ppermute | solution.py:327
  20.0 3.7 %collective-permute-start.10 = (bf16[256,512]{1,0:T(8,128)(2,1)S(1)}, bf16[256,512]{1,0:T(8,128)(2,1)S(1)}, u32[]{:S(2)}, u32[]{:S(2)}) collective-permute-start(bf16[256,512]{1,0:T(8,128)(2,1)S(1)} %collective-permute-done.4.refs_3_), channel_id=1, source_target_pairs={{0,1},{1,0},{2,3},{3,2},{4,5},{5,4},{6,7},{7,6},{8,9},{9,8},{10,11... | collective-permute-start | bytes 786440 | tf_op jit(solution)/shard_map/ppermute | solution.py:327
  20.1 3.6 %collective-permute-start.7 = (f32[4,128]{1,0:T(4,128)S(1)}, f32[4,128]{1,0:T(4,128)S(1)}, u32[]{:S(2)}, u32[]{:S(2)}) collective-permute-start(f32[4,128]{1,0:T(4,128)S(1)} %add.27.jitter_ref), channel_id=1, source_target_pairs={{0,16},{8,24},{16,0},{24,8},{1,17},{9,25},{17,1},{25,9},{2,18},{10... | collective-permute-start | bytes 6152 | tf_op jit(solution)/shard_map/ppermute | solution.py:329
  22.5 1.2 %copy-start.2 = (s32[1024]{0:T(1024)S(1)}, s32[1024]{0:T(1024)}, u32[]{:S(2)}) copy-start(s32[1024]{0:T(1024)} %param.8) | copy-start | bytes 12292

commit v3 on v2

--- a/solution.py
+++ b/solution.py
@@ -2,7 +2,6 @@
 
 import jax
 import jax.numpy as jnp
-import ml_dtypes
 import numpy as np
 from jax import lax
 from jax.experimental import pallas as pl
@@ -25,24 +24,11 @@
     return lax.dot_general(a, b, NN, precision=lax.Precision.HIGHEST, preferred_element_type=F32)
 
 
-def frequencies(length):
-    period = length + MAXLAG
-    return 2 * np.pi / period * (np.arange(period // 2) + 0.5)
-
-
-def angle_parts(length, group):
-    width = length + MAXLAG
-    first, time = frequencies(length)[:group], np.arange(length)
-    stride = frequencies(length)[::group] - first[0]
-    column = np.repeat(frequencies(length).reshape(-1, 1, group), 2, 1).reshape(-1)
-    parts = []
-    for angle in (stride[:, None] * time, first[:, None] * time):
-        parts += [np.pad(table, ((0, 0), (0, MAXLAG))) for table in (np.cos(angle), np.sin(angle))]
-    for lag in (np.arange(-MAXLAG, MAXLAG, 8), np.arange(8)):
-        angle = lag[:, None] * column
-        parts += [np.cos(angle), np.sin(angle)]
-    assert all(part.shape[1] == width for part in parts)
-    return np.concatenate([np.pad(p, ((0, -p.shape[0] % 8), (0, 0))) for p in parts]).astype(np.float32)
+def turns(first, second, period):
+    product = (first * second).astype(F32)
+    whole = jnp.floor((product + 0.5) * F32(0.5 / period))
+    angle = (product - whole * F32(2 * period) - F32(period)) * F32(np.pi / period)
+    return -jnp.cos(angle), -jnp.sin(angle)
 
 
 def store_halves(ref, rows, value, times):
@@ -53,8 +39,9 @@
     ref[rows] = jnp.concatenate(order, 1)
 
 
-def prepare_kernel(half, group, taps, parts, matrix_t, table, inverse):
+def fill_tables(taps, matrix_t, table, inverse, half, group):
     length = matrix_t.shape[0]
+    period = length + MAXLAG
     row = jnp.concatenate([taps[...].astype(F32), jnp.zeros((1, length - taps.shape[1]), F32)], 1)
     spread = jnp.broadcast_to(row, (length, length))
     rolled = pltpu.roll(spread, length - half, 1, stride=1, stride_axis=0).T
@@ -63,28 +50,40 @@
     )
     matrix_t[...] = jnp.where(jnp.abs(distance) <= half, rolled, 0.0).astype(matrix_t.dtype)
 
-    groups = (length + MAXLAG) // 2 // group
+    def iota(shape, dim):
+        return lax.broadcasted_iota(jnp.int32, shape, dim)
+
+    groups = period // 2 // group
     padded = groups + -groups % 8
-    cos_first, sin_first = (parts[2 * padded + i * group : 2 * padded + (i + 1) * group, 0:length] for i in range(2))
+    cos_first, sin_first = turns(2 * iota((group, length), 0) + 1, iota((group, length), 1), period)
+    cos_steps, sin_steps = turns(2 * group * iota((padded, length), 0), iota((padded, length), 1), period)
     for g in range(groups):
-        cos_step, sin_step = parts[g : g + 1, 0:length], parts[padded + g : padded + g + 1, 0:length]
+        cos_step, sin_step = cos_steps[g : g + 1], sin_steps[g : g + 1]
         real = cos_first * cos_step - sin_first * sin_step
         imag = -(sin_first * cos_step + cos_first * sin_step)
         store_halves(table, pl.ds(2 * g * group, 2 * group), jnp.concatenate([real, imag], 0), 2)
 
-    base = 2 * padded + 2 * group
     steps = LAGS // 8
-    cos_first, sin_first = (parts[base + 2 * steps + 8 * i : base + 2 * steps + 8 * (i + 1), :] for i in range(2))
-    lane = lax.broadcasted_iota(jnp.int32, (8, length + MAXLAG), 1)
-    is_real = (lane & group) == 0
-    scale = F32(2.0 / (length + MAXLAG))
+    half_period = period // 2
+
+    def odd(rows):
+        return 2 * iota((rows, half_period), 1) + 1
+
+    cos_first, sin_first = turns(odd(8), iota((8, half_period), 0), period)
+    cos_steps, sin_steps = turns(odd(steps), 8 * iota((steps, half_period), 0) + 2 * period - MAXLAG, period)
+    scale = F32(2.0 / period)
+    cos_steps, sin_steps = cos_steps * scale, sin_steps * scale
     for step in range(steps):
-        cos_step = parts[base + step : base + step + 1, :] * scale
-        sin_step = parts[base + steps + step : base + steps + step + 1, :] * scale
+        cos_step, sin_step = cos_steps[step : step + 1], sin_steps[step : step + 1]
         cosine = cos_first * cos_step - sin_first * sin_step
         sine = sin_first * cos_step + cos_first * sin_step
-        store_halves(inverse, pl.ds(8 * step, 8), jnp.where(is_real, cosine, -sine), 3)
-        store_halves(inverse, pl.ds(LAGS + 8 * step, 8), jnp.where(is_real, sine, cosine), 3)
+        store_halves(inverse, pl.ds(8 * step, 8), cosine, 3)
+        store_halves(inverse, pl.ds(LAGS + 8 * step, 8), sine, 3)
+
+
+def first_kernel(half, group, width, residues, taps, mine, mate, matrix_t, table, inverse, out):
+    fill_tables(taps, matrix_t, table, inverse, half, group)
+    block_kernel(width, residues, matrix_t, table, mine, mate, out)
 
 
 def transform(records, matrix_t, table, width, residues):
@@ -98,12 +97,14 @@
     return dot(table, jnp.concatenate([filtered, filtered], 0)).astype(BF16)
 
 
-def block_kernel(width, residues, matrix_t, table, mine, mate, out):
-    records = jnp.concatenate([mine[...], mate[...]], 0)
-    spectra = transform(records, matrix_t[...], table[...], width, residues)
-    lanes = out.shape[2]
-    for index in range(out.shape[0]):
-        out[index] = spectra[:, index * lanes : (index + 1) * lanes]
+def block_kernel(width, residues, matrix_t, table, *refs):
+    count = len(refs) // 3
+    for mine, mate, out in zip(refs[:count], refs[count : 2 * count], refs[2 * count :]):
+        records = jnp.concatenate([mine[...], mate[...]], 0)
+        spectra = transform(records, matrix_t[...], table[...], width, residues)
+        lanes = out.shape[2]
+        for index in range(out.shape[0]):
+            out[index] = spectra[:, index * lanes : (index + 1) * lanes]
 
 
 def bin_lanes(product, first_row, rows_per, group, rows_q):
@@ -134,10 +135,10 @@
 
 def late_kernel(
     width, residues, segs, length, src_count,
-    jitter_ref, arrived, bin_order, matrix_t, table, inverse, *refs,
+    bin_order, matrix_t, table, inverse, *refs,
 ):
-    early, refs = refs[: src_count - 1], refs[src_count - 1 :]
-    mine, mate, out, spectra, edges, shifted, binned = refs
+    jitters, early, refs = refs[:2], refs[2 : src_count + 1], refs[src_count + 1 :]
+    *pieces, out, spectra, edges, shifted, binned = refs
     src = lax.axis_index("src")
     owned = out.shape[0]
     rank = lax.axis_index(("src", "rcv", "seg"))
@@ -161,7 +162,7 @@
     for q in range(rows_q):
         spectra[1 + q, height : height + 16] = one
 
-    jitter = jitter_ref[...] + arrived[...]
+    jitter = sum(ref[...] for ref in jitters)
     blocks, block_lanes = jitter.shape
     edges[...] = jnp.zeros_like(edges)
     source_lane = lax.broadcasted_iota(jnp.int32, (block_lanes, lanes), 0)
@@ -191,7 +192,7 @@
     here_bf = here.astype(BF16)
     difference = here - after
 
-    records = jnp.concatenate([mine[...], mate[...]], 0)
+    records = jnp.concatenate([piece[...] for piece in pieces], 0)
     fresh = transform(records, matrix_t[...], table[...], width, residues)
     for index in range(per_block):
         spectra[1 + per_block * (src ^ last) + index, 0:height] = fresh[:, index * lanes : (index + 1) * lanes]
@@ -207,6 +208,14 @@
 
     upper = jitter_rows.astype(BF16)
     lower = (1.0 - jitter_rows).astype(BF16)
+
+    swap = (lax.broadcasted_iota(jnp.int32, (height // 2, 128), 1) & group) == 0
+
+    def cross(imag):
+        tiles = [imag[:, 128 * i : 128 * (i + 1)] for i in range(4)]
+        return jnp.concatenate(
+            [jnp.where(swap, pltpu.roll(tile, 128 - group, 1), -pltpu.roll(tile, group, 1)) for tile in tiles], 1
+        )
 
     def one_group(g, carry):
         rows = pl.ds(pl.multiple_of(g * step, step), step)
@@ -216,9 +225,9 @@
             left.append(jnp.concatenate([values * lower[q : q + 1], values * upper[q : q + 1]], 1))
         right = [shifted[p, rows] for p in range(rows_q + 1)]
         product = dot(jnp.concatenate(right, 0), jnp.concatenate(left, 0), NT)
-        binned[rows] = jnp.concatenate(
-            [bin_lanes(product, part * group, step, group, rows_q) for part in range(2)], 0
-        )
+        for part in range(2):
+            place = pl.ds(pl.multiple_of(g * group, group), group)
+            binned[part, place] = bin_lanes(product, part * group, step, group, rows_q)
         return carry
 
     lax.fori_loop(0, height // step, one_group, 0, unroll=UNROLL)
@@ -233,7 +242,7 @@
         counted = jnp.concatenate([counted[16 * p : 16 * p + 16] for p in range(rows_q + 1)], 0)
     counts = jnp.sum(bin_lanes(counted, 0, 16, group, rows_q), 0, keepdims=True)
 
-    values = binned[...]
+    values = binned[0] + cross(binned[1])
     high = values.astype(BF16)
     low = (values - high.astype(F32)).astype(BF16)
     lagged = dot(inverse[...], jnp.concatenate([high, low, high], 0))
@@ -276,58 +285,70 @@
     owned = bin_order.shape[0] // owners
 
     mine = traces.reshape(seg_local * width, length)
+    def to_mate(piece):
+        return lax.ppermute(piece, "seg", partners("seg", 1))
+
     received = [mine] + [lax.ppermute(mine, "src", partners("src", k)) for k in range(1, src_count)]
-    mates = [lax.ppermute(mine, "seg", partners("seg", 1))]
+    mates = [to_mate(mine)]
 
     src, rcv = lax.axis_index("src"), lax.axis_index("rcv")
-    receivers = pair_bins.shape[1]
-    jitter = pair_bins[width - 1 : width, :] - (
-        rcv * receivers + jnp.arange(receivers, dtype=jnp.int32)[None, :]
-    )
+    assert src_count == rcv_count
+    channel = jnp.arange(width, dtype=jnp.int32)[None, :]
+    of_receivers = pair_bins[width - 1 : width, :] - (rcv * width + channel)
+    of_sources = channels - (src * width + channel) - pair_bins[:, 0:1].reshape(1, width)
     slots = jnp.arange(rcv_count, dtype=jnp.int32)[:, None]
-    jitter = jnp.where((slots == rcv) & (src == src_count - 1), jitter, 0).astype(F32)
+    jitter = jnp.where((slots == rcv) & (src == src_count - 1), of_receivers, 0)
+    jitter = (jitter + jnp.where((slots == src) & (rcv == 0), of_sources, 0)).astype(F32)
 
     vmem = pl.BlockSpec(memory_space=pltpu.VMEM)
     last = src_count - 1
     per_block = width // residues
     params = pltpu.CompilerParams(vmem_limit_bytes=(20 if lanes <= 128 else 40) * 2**20)
     group = 128 // rows_q
-    matrix_t, table, inverse = pl.pallas_call(
-        functools.partial(prepare_kernel, fir_taps.shape[0] // 2, group),
+    matrix_t, table, inverse, first = pl.pallas_call(
+        functools.partial(first_kernel, fir_taps.shape[0] // 2, group, width, residues),
         out_shape=[
             jax.ShapeDtypeStruct((length, length), BF16),
             jax.ShapeDtypeStruct((period, 2 * length), BF16),
-            jax.ShapeDtypeStruct((2 * LAGS, 3 * period), BF16),
+            jax.ShapeDtypeStruct((2 * LAGS, 3 * period // 2), BF16),
+            jax.ShapeDtypeStruct((per_block, period, lanes), BF16),
         ],
-        in_specs=[vmem] * 2,
-        out_specs=[vmem] * 3,
+        in_specs=[vmem] * 3,
+        out_specs=[vmem] * 4,
         compiler_params=params,
         cost_estimate=cost(0.01),
-        name="prepare",
-    )(fir_taps[None, :], jnp.asarray(angle_parts(length, group)))
-
-    def block_spectra(k):
+        name="tables_and_own_spectra",
+    )(fir_taps[None, :], mine, mates[0])
+
+    def block_spectra(blocks):
         return pl.pallas_call(
             functools.partial(block_kernel, width, residues),
-            out_shape=jax.ShapeDtypeStruct((per_block, period, lanes), BF16),
-            in_specs=[vmem] * 4,
-            out_specs=vmem,
+            out_shape=[jax.ShapeDtypeStruct((per_block, period, lanes), BF16) for _ in blocks],
+            in_specs=[vmem] * (2 + 2 * len(blocks)),
+            out_specs=[vmem] * len(blocks),
             compiler_params=params,
             cost_estimate=cost(0.01),
             name="block_spectra",
-        )(matrix_t, table, received[k], mates[k])
-
-    hops = [("rcv", 1 << bit) for bit in range((rcv_count - 1).bit_length())]
-    hops += [("src", 1 << bit) for bit in range((src_count - 1).bit_length())]
+        )(matrix_t, table, *[received[k] for k in blocks], *[mates[k] for k in blocks])
+
+    bits = [1 << bit for bit in range(1, (src_count - 1).bit_length())]
+    hops = [(0, bit) for bit in bits] + [(1, 1)] + [(bit, 0) for bit in bits]
     arrived = jnp.zeros_like(jitter)
-    early = [block_spectra(0)]
-    for turn, (axis, step) in enumerate(hops):
+    for turn, (over_src, over_rcv) in enumerate(hops):
+        if turn == len(hops) - 2:
+            arrived, first = lax.optimization_barrier((arrived, first))
         if turn == len(hops) - 1:
-            *received[1:], early[0], arrived = lax.optimization_barrier((*received[1:], early[0], arrived))
-            mates += [lax.ppermute(block, "seg", partners("seg", 1)) for block in received[1:]]
+            *received[1:], first, arrived = lax.optimization_barrier((*received[1:], first, arrived))
         jitter = jitter + arrived
-        arrived = lax.ppermute(jitter, axis, partners(axis, step))
-    early += [block_spectra(k) for k in range(1, last)]
+        pairs = [
+            (i * rcv_count + z, (i ^ over_src) * rcv_count + (z ^ over_rcv))
+            for i in range(src_count)
+            for z in range(rcv_count)
+        ]
+        arrived = lax.ppermute(jitter, ("src", "rcv"), pairs)
+    jitters = [jitter, arrived]
+    mates += [to_mate(block) for block in received[1:]]
+    early = [first, *block_spectra(range(1, last))]
     return pl.pallas_call(
         functools.partial(late_kernel, width, residues, segs, length, src_count),
         out_shape=jax.ShapeDtypeStruct((owned, LAGS), F32),
@@ -337,12 +358,12 @@
             pltpu.VMEM((rows_q + 2, period + 16, lanes), BF16),
             pltpu.VMEM((32, lanes), F32),
             pltpu.VMEM((rows_q + 1, period + 16, 2 * lanes), BF16),
-            pltpu.VMEM((period, 512), F32),
+            pltpu.VMEM((2, period // 2, 512), F32),
         ],
         compiler_params=params,
         cost_estimate=cost(0.01),
         name="bin_stacks",
-    )(jitter, arrived, bin_order.reshape(-1, 128), matrix_t, table, inverse, *early, received[last], mates[last])
+    )(bin_order.reshape(-1, 128), matrix_t, table, inverse, *jitters, *early, received[last], mates[last])
 
 
 def solution(mesh):

time: 30.3 us -> 27.9 us (0.921)
  waiting for transfers between devices: 3.46 us -> 2 us
  Pallas kernels: 10.5 us -> 10 us
  starting transfers between devices: 12.5 us -> 12.1 us
    ppermute x8 -> x7, waiting for transfers between devices: 3.45 us -> 0.71 us  [the longest x3 0.7 us: on_device(): arrived = lax.ppermute(jitter, ('src', 'rcv'), pairs)]
    ppermute x8 -> x7, starting transfers between devices: 9.02 us -> 7.6 us  [the longest x3 7.09 us: on_device(): arrived = lax.ppermute(jitter, ('src', 'rcv'), pairs)]
    pallas_call x3 -> x1, Pallas kernels: 3.45 us -> 2.11 us  [block_spectra(): pl.pallas_call(functools.partial(block_kernel, width, residues), out_shap...]
    ppermute x3, waiting for transfers between devices: 0.01 us -> 1.28 us  [on_device(): lax.ppermute(mine, 'src', partners('src', k))]
    unnamed x8 -> x6, local copies, waits for them, and re-layouts: 2.59 us -> 1.61 us
    ppermute x3, starting transfers between devices: 3.49 us -> 4.46 us  [on_device(): lax.ppermute(mine, 'src', partners('src', k))]
    slice x0 -> x1, local copies, waits for them, and re-layouts: none -> 0.94 us  [on_device(): pair_bins[:, 0:1].reshape(1, width)]
    pallas_call x1, Pallas kernels: 0.67 us -> 1.56 us  [on_device(): pl.pallas_call(functools.partial(first_kernel, fir_taps.shape[0] // 2, gr...]
  transfers between devices with their start and end apart: 11 -> 10, of which waited for: 2 -> 3; matrix products, arithmetic and copies ran while one was open for 0% -> 7% of each run, Pallas kernels for 14% -> 13%
where the time goes in v3:
time: 27.9 us; the launch traced here: 27.7 us
  starting transfers between devices  12.1 us (43%)
  Pallas kernels  10 us (36%)
  local copies, waits for them, and re-layouts  2.55 us (9%)
  waiting for transfers between devices  2 us (7%)
  other arithmetic  0.94 us (3%)
    ppermute x3, starting transfers between devices, on_device(): arrived = lax.ppermute(jitter, ('src', 'rcv'), pairs)  7.09 us
    pallas_call x1, Pallas kernels, on_device(): pl.pallas_call(functools.partial(late_kernel, width, residues, segs, leng...  6.36 us
    ppermute x3, starting transfers between devices, on_device(): lax.ppermute(mine, 'src', partners('src', k))  4.46 us
    pallas_call x1, Pallas kernels, block_spectra(): pl.pallas_call(functools.partial(block_kernel, width, residues), out_shap...  2.11 us
    unnamed x6, local copies, waits for them, and re-layouts  1.61 us
    pallas_call x1, Pallas kernels, on_device(): pl.pallas_call(functools.partial(first_kernel, fir_taps.shape[0] // 2, gr...  1.56 us
    ppermute x3, waiting for transfers between devices, on_device(): lax.ppermute(mine, 'src', partners('src', k))  1.28 us
    slice x1, local copies, waits for them, and re-layouts, on_device(): pair_bins[:, 0:1].reshape(1, width)  0.94 us
  transfers between devices with their start and end apart: 10, of which 3 were waited for; matrix products, arithmetic and copies ran while one was open for 7% of the time, Pallas kernels for 13%

profile of v3, /device:TPU:0, one launch (start us, length us, event | category | flops | bytes accessed | tf_op | source)
XLA Modules:
  0.0 27.7 jit_solution(940476640646404196)
XLA Ops:
  0.0 3.9 %collective-permute-start.4 = (bf16[256,512]{1,0:T(8,128)(2,1)}, bf16[256,512]{1,0:T(8,128)(2,1)S(1)}, u32[]{:S(2)}, u32[]{:S(2)}) collective-permute-start(bf16[256,512]{1,0:T(8,128)(2,1)} %bitcast.5), channel_id=1, source_target_pairs={{0,24},{8,16},{16,8},{24,0},{1,25},{9,17},{17,9},{25,1},{2,26},{10... | collective-permute-start | bytes 786440 | tf_op jit(solution)/shard_map/ppermute | solution.py:291
  3.9 0.5 %collective-permute-start.3 = (bf16[256,512]{1,0:T(8,128)(2,1)}, bf16[256,512]{1,0:T(8,128)(2,1)S(1)}, u32[]{:S(2)}, u32[]{:S(2)}) collective-permute-start(bf16[256,512]{1,0:T(8,128)(2,1)} %bitcast.6), channel_id=1, source_target_pairs={{0,16},{8,24},{16,0},{24,8},{1,17},{9,25},{17,1},{25,9},{2,18},{10... | collective-permute-start | bytes 786440 | tf_op jit(solution)/shard_map/ppermute | solution.py:291
  4.4 0.1 collective-permute-start.2
  4.5 0.0 collective-permute-start
  4.5 0.9 %slice_reduce_fusion = s32[128]{0:T(128)S(1)} fusion(s32[128,128]{1,0:T(8,128)} %param.6), kind=kLoop, calls=%fused_computation | loop fusion | bytes 1024 | tf_op jit(solution)/shard_map/slice | solution.py:298
  5.4 0.7 %subtract_bitcast_fusion = s32[128]{0:T(128)S(1)} fusion(s32[128,128]{1,0:T(8,128)} %param.6, s32[]{:T(128)S(6)} %mul.6), kind=kLoop, calls=%fused_computation.5 | loop fusion | flops 256 | bytes 1028 | tf_op jit(solution)/shard_map/jit(_where)/broadcast_in_dim | solution.py:300
  6.1 0.1 add_convert_fusion
  6.2 3.1 %collective-permute-start.1 = (f32[4,128]{1,0:T(4,128)S(1)}, f32[4,128]{1,0:T(4,128)S(1)}, u32[]{:S(2)}, u32[]{:S(2)}) collective-permute-start(f32[4,128]{1,0:T(4,128)S(1)} %add_convert_fusion), channel_id=1, source_target_pairs={{0,4},{2,6},{4,0},{6,2},{8,12},{10,14},{12,8},{14,10},{16,20},{18,... | collective-permute-start | bytes 6152 | tf_op jit(solution)/shard_map/ppermute | solution.py:348
  9.3 0.0 collective-permute-done.mate
  9.3 0.0 copy-start
  9.3 0.9 %copy-done = bf16[2,128,512]{2,1,0:T(8,128)(2,1)S(1)} copy-done((bf16[2,128,512]{2,1,0:T(8,128)(2,1)S(1)}, bf16[2,128,512]{2,1,0:T(8,128)(2,1)}, u32[]{:S(2)}) %copy-start) | copy-done | bytes 262168
  10.2 0.0 copy-start.2
  10.2 0.7 %copy-done.2 = bf16[31]{0:T(256)(128)(2,1)S(1)} copy-done((bf16[31]{0:T(256)(128)(2,1)S(1)}, bf16[31]{0:T(256)(128)(2,1)}, u32[]{:S(2)}) %copy-start.2) | copy-done | bytes 86
  10.9 1.6 %tables_and_own_spectra.1 = (bf16[512,512]{1,0:T(8,128)(2,1)S(1)}, bf16[576,1024]{1,0:T(8,128)(2,1)S(1)}, bf16[256,864]{1,0:T(8,128)(2,1)S(1)}, bf16[4,576,128]{2,1,0:T(8,128)(2,1)S(1)}) custom-call(bf16[1,31]{1,0:T(2,128)(2,1)S(1)} %bitcast.11, bf16[256,512]{1,0:T(8,128)(2,1)S(1)} %bitcast.9, bf16[256,512]{1,0:T(8,128)(2,1)S(1)} %collective-permute-done.mate), custom_call_target="tpu_custom_call" | custom-call | flops 10000000 | bytes 30000 | tf_op jit(solution)/shard_map/tables_and_own_spectra/pallas_call | solution.py:308
  12.5 0.0 collective-permute-done.1
  12.5 0.1 fusion
  12.5 2.5 %collective-permute-start.5 = (f32[4,128]{1,0:T(4,128)S(1)}, f32[4,128]{1,0:T(4,128)S(1)}, u32[]{:S(2)}, u32[]{:S(2)}) collective-permute-start(f32[4,128]{1,0:T(4,128)S(1)} %fusion), channel_id=1, source_target_pairs={{0,10},{2,8},{4,14},{6,12},{8,2},{10,0},{12,6},{14,4},{16,26},{18,... | collective-permute-start | bytes 6152 | tf_op jit(solution)/shard_map/ppermute | solution.py:348
  15.0 0.0 collective-permute-done.4.refs_5_
  15.1 1.0 %collective-permute-done.3.refs_1_ = bf16[256,512]{1,0:T(8,128)(2,1)S(1)} collective-permute-done((bf16[256,512]{1,0:T(8,128)(2,1)}, bf16[256,512]{1,0:T(8,128)(2,1)S(1)}, u32[]{:S(2)}, u32[]{:S(2)}) %collective-permute-start.3) | collective-permute-done | bytes 262176 | tf_op jit(solution)/shard_map/ppermute | solution.py:291
  16.0 0.3 %collective-permute-done.2.refs_0_ = bf16[256,512]{1,0:T(8,128)(2,1)S(1)} collective-permute-done((bf16[256,512]{1,0:T(8,128)(2,1)}, bf16[256,512]{1,0:T(8,128)(2,1)S(1)}, u32[]{:S(2)}, u32[]{:S(2)}) %collective-permute-start.2) | collective-permute-done | bytes 262176 | tf_op jit(solution)/shard_map/ppermute | solution.py:291
  16.3 0.7 %collective-permute-done.5 = f32[4,128]{1,0:T(4,128)S(1)} collective-permute-done((f32[4,128]{1,0:T(4,128)S(1)}, f32[4,128]{1,0:T(4,128)S(1)}, u32[]{:S(2)}, u32[]{:S(2)}) %collective-permute-start.5) | collective-permute-done | bytes 2080 | tf_op jit(solution)/shard_map/ppermute | solution.py:348
  17.0 0.0 collective-permute-start.7
  17.0 0.5 %collective-permute-start.8 = (bf16[256,512]{1,0:T(8,128)(2,1)S(1)}, bf16[256,512]{1,0:T(8,128)(2,1)S(1)}, u32[]{:S(2)}, u32[]{:S(2)}) collective-permute-start(bf16[256,512]{1,0:T(8,128)(2,1)S(1)} %collective-permute-done.3.refs_1_), channel_id=1, source_target_pairs={{0,1},{1,0},{2,3},{3,2},{4,5},{5,4},{6,7},{7,6},{8,9},{9,8},{10,11... | collective-permute-start | bytes 786440 | tf_op jit(solution)/shard_map/ppermute | solution.py:289
  17.5 0.0 collective-permute-start.9
  17.5 0.1 fusion.1.refs_0_
  17.6 1.5 %collective-permute-start.6 = (f32[4,128]{1,0:T(4,128)S(1)}, f32[4,128]{1,0:T(4,128)S(1)}, u32[]{:S(2)}, u32[]{:S(2)}) collective-permute-start(f32[4,128]{1,0:T(4,128)S(1)} %fusion.1.refs_0_), channel_id=1, source_target_pairs={{0,16},{2,18},{4,20},{6,22},{8,24},{10,26},{12,28},{14,30},{16,0},... | collective-permute-start | bytes 6152 | tf_op jit(solution)/shard_map/ppermute | solution.py:348
  19.1 0.0 collective-permute-done.7.refs_2_
  19.1 0.0 collective-permute-done.8.refs_3_
  19.1 0.0 copy-start.1
  19.1 2.1 %block_spectra.1 = (bf16[4,576,128]{2,1,0:T(8,128)(2,1)S(1)}, bf16[4,576,128]{2,1,0:T(8,128)(2,1)S(1)}) custom-call(bf16[512,512]{1,0:T(8,128)(2,1)S(1)} %get-tuple-element.18.matrix_t, bf16[576,1024]{1,0:T(8,128)(2,1)S(1)} %get-tuple-element.19.table, bf16[256,512]{1,0:T(8,128)(2,1)S(1)} %collective-permute-done.2.refs_0_, ...), custom_call_target="tpu_custom_call" | custom-call | flops 10000000 | bytes 30000 | tf_op jit(solution)/shard_map/block_spectra/pallas_call | solution.py:324
  21.3 0.0 collective-permute-done.6.refs_1_
  21.3 0.0 collective-permute-done.9.refs_6_
  21.3 0.0 copy-done.1
  21.3 6.4 %bin_stacks.1 = f32[32,128]{1,0:T(8,128)} custom-call(s32[8,128]{1,0:T(8,128)S(1)} %bitcast.10, bf16[512,512]{1,0:T(8,128)(2,1)S(1)} %get-tuple-element.18.matrix_t, bf16[576,1024]{1,0:T(8,128)(2,1)S(1)} %get-tuple-element.19.table, bf16[256,864]{1,0:T(8,128)(2,1)S(1)} %get-tuple-element.20.inverse, f32[4,128]{1,0:T(4,128)S(1)} %fusion.1.refs_0_, ...), custom_call_target="tpu_custom_call" | custom-call | flops 10000000 | bytes 30000 | tf_op jit(solution)/shard_map/bin_stacks/pallas_call | solution.py:352
  (2 shorter events, 0.0 us)
Async XLA Ops:
  0.0 15.1 %collective-permute-start.4 = (bf16[256,512]{1,0:T(8,128)(2,1)}, bf16[256,512]{1,0:T(8,128)(2,1)S(1)}, u32[]{:S(2)}, u32[]{:S(2)}) collective-permute-start(bf16[256,512]{1,0:T(8,128)(2,1)} %bitcast.5), channel_id=1, source_target_pairs={{0,24},{8,16},{16,8},{24,0},{1,25},{9,17},{17,9},{25,1},{2,26},{10... | collective-permute-start | bytes 786440 | tf_op jit(solution)/shard_map/ppermute | solution.py:291
  3.9 12.1 %collective-permute-start.3 = (bf16[256,512]{1,0:T(8,128)(2,1)}, bf16[256,512]{1,0:T(8,128)(2,1)S(1)}, u32[]{:S(2)}, u32[]{:S(2)}) collective-permute-start(bf16[256,512]{1,0:T(8,128)(2,1)} %bitcast.6), channel_id=1, source_target_pairs={{0,16},{8,24},{16,0},{24,8},{1,17},{9,25},{17,1},{25,9},{2,18},{10... | collective-permute-start | bytes 786440 | tf_op jit(solution)/shard_map/ppermute | solution.py:291
  4.4 11.9 %collective-permute-start.2 = (bf16[256,512]{1,0:T(8,128)(2,1)}, bf16[256,512]{1,0:T(8,128)(2,1)S(1)}, u32[]{:S(2)}, u32[]{:S(2)}) collective-permute-start(bf16[256,512]{1,0:T(8,128)(2,1)} %bitcast.7), channel_id=1, source_target_pairs={{0,8},{8,0},{16,24},{24,16},{1,9},{9,1},{17,25},{25,17},{2,10},{10... | collective-permute-start | bytes 786440 | tf_op jit(solution)/shard_map/ppermute | solution.py:291
  4.5 4.8 %collective-permute-start = (bf16[256,512]{1,0:T(8,128)(2,1)}, bf16[256,512]{1,0:T(8,128)(2,1)S(1)}, u32[]{:S(2)}, u32[]{:S(2)}) collective-permute-start(bf16[256,512]{1,0:T(8,128)(2,1)} %bitcast.8), channel_id=1, source_target_pairs={{0,1},{1,0},{2,3},{3,2},{4,5},{5,4},{6,7},{7,6},{8,9},{9,8},{10,11... | collective-permute-start | bytes 786440 | tf_op jit(solution)/shard_map/ppermute | solution.py:289
  6.2 6.3 %collective-permute-start.1 = (f32[4,128]{1,0:T(4,128)S(1)}, f32[4,128]{1,0:T(4,128)S(1)}, u32[]{:S(2)}, u32[]{:S(2)}) collective-permute-start(f32[4,128]{1,0:T(4,128)S(1)} %add_convert_fusion), channel_id=1, source_target_pairs={{0,4},{2,6},{4,0},{6,2},{8,12},{10,14},{12,8},{14,10},{16,20},{18,... | collective-permute-start | bytes 6152 | tf_op jit(solution)/shard_map/ppermute | solution.py:348
  9.3 1.0 %copy-start = (bf16[2,128,512]{2,1,0:T(8,128)(2,1)S(1)}, bf16[2,128,512]{2,1,0:T(8,128)(2,1)}, u32[]{:S(2)}) copy-start(bf16[2,128,512]{2,1,0:T(8,128)(2,1)} %param.4) | copy-start | bytes 786436
  10.2 0.7 %copy-start.2 = (bf16[31]{0:T(256)(128)(2,1)S(1)}, bf16[31]{0:T(256)(128)(2,1)}, u32[]{:S(2)}) copy-start(bf16[31]{0:T(256)(128)(2,1)} %param.5) | copy-start | bytes 190
  12.5 4.5 %collective-permute-start.5 = (f32[4,128]{1,0:T(4,128)S(1)}, f32[4,128]{1,0:T(4,128)S(1)}, u32[]{:S(2)}, u32[]{:S(2)}) collective-permute-start(f32[4,128]{1,0:T(4,128)S(1)} %fusion), channel_id=1, source_target_pairs={{0,10},{2,8},{4,14},{6,12},{8,2},{10,0},{12,6},{14,4},{16,26},{18,... | collective-permute-start | bytes 6152 | tf_op jit(solution)/shard_map/ppermute | solution.py:348
  17.0 2.1 %collective-permute-start.7 = (bf16[256,512]{1,0:T(8,128)(2,1)S(1)}, bf16[256,512]{1,0:T(8,128)(2,1)S(1)}, u32[]{:S(2)}, u32[]{:S(2)}) collective-permute-start(bf16[256,512]{1,0:T(8,128)(2,1)S(1)} %collective-permute-done.2.refs_0_), channel_id=1, source_target_pairs={{0,1},{1,0},{2,3},{3,2},{4,5},{5,4},{6,7},{7,6},{8,9},{9,8},{10,11... | collective-permute-start | bytes 786440 | tf_op jit(solution)/shard_map/ppermute | solution.py:289
  17.0 2.1 %collective-permute-start.8 = (bf16[256,512]{1,0:T(8,128)(2,1)S(1)}, bf16[256,512]{1,0:T(8,128)(2,1)S(1)}, u32[]{:S(2)}, u32[]{:S(2)}) collective-permute-start(bf16[256,512]{1,0:T(8,128)(2,1)S(1)} %collective-permute-done.3.refs_1_), channel_id=1, source_target_pairs={{0,1},{1,0},{2,3},{3,2},{4,5},{5,4},{6,7},{7,6},{8,9},{9,8},{10,11... | collective-permute-start | bytes 786440 | tf_op jit(solution)/shard_map/ppermute | solution.py:289
  17.5 3.7 %collective-permute-start.9 = (bf16[256,512]{1,0:T(8,128)(2,1)S(1)}, bf16[256,512]{1,0:T(8,128)(2,1)S(1)}, u32[]{:S(2)}, u32[]{:S(2)}) collective-permute-start(bf16[256,512]{1,0:T(8,128)(2,1)S(1)} %collective-permute-done.4.refs_5_), channel_id=1, source_target_pairs={{0,1},{1,0},{2,3},{3,2},{4,5},{5,4},{6,7},{7,6},{8,9},{9,8},{10,11... | collective-permute-start | bytes 786440 | tf_op jit(solution)/shard_map/ppermute | solution.py:289
  17.6 3.6 %collective-permute-start.6 = (f32[4,128]{1,0:T(4,128)S(1)}, f32[4,128]{1,0:T(4,128)S(1)}, u32[]{:S(2)}, u32[]{:S(2)}) collective-permute-start(f32[4,128]{1,0:T(4,128)S(1)} %fusion.1.refs_0_), channel_id=1, source_target_pairs={{0,16},{2,18},{4,20},{6,22},{8,24},{10,26},{12,28},{14,30},{16,0},... | collective-permute-start | bytes 6152 | tf_op jit(solution)/shard_map/ppermute | solution.py:348
  19.1 2.1 %copy-start.1 = (s32[1024]{0:T(1024)S(1)}, s32[1024]{0:T(1024)}, u32[]{:S(2)}) copy-start(s32[1024]{0:T(1024)} %param.7) | copy-start | bytes 12292

commit v4 on v3

--- a/solution.py
+++ b/solution.py
@@ -14,6 +14,7 @@
 NT = (((1,), (1,)), ((), ()))
 NN = (((1,), (0,)), ((), ()))
 UNROLL = 36
+BAND = 16
 
 
 def dot(a, b, dims=NN):
@@ -93,7 +94,14 @@
         for first in range(0, width, residues)
         for s in range(segs)
     ]
-    filtered = dot(matrix_t, jnp.concatenate(rows, 0), NT).astype(BF16)
+    rows = jnp.concatenate(rows, 0)
+    middle = rows.shape[1] // 2
+    start, stop = middle - BAND, middle + BAND
+    early = dot(matrix_t[0:stop, 0:middle], rows[:, 0:middle], NT)
+    late = dot(matrix_t[start:, middle:], rows[:, middle:], NT)
+    filtered = jnp.concatenate(
+        [early[0:start], early[start:stop] + late[0 : 2 * BAND], late[2 * BAND :]], 0
+    ).astype(BF16)
     return dot(table, jnp.concatenate([filtered, filtered], 0)).astype(BF16)
 
 
@@ -292,7 +300,7 @@
     mates = [to_mate(mine)]
 
     src, rcv = lax.axis_index("src"), lax.axis_index("rcv")
-    assert src_count == rcv_count
+    assert src_count == rcv_count and fir_taps.shape[0] // 2 <= BAND
     channel = jnp.arange(width, dtype=jnp.int32)[None, :]
     of_receivers = pair_bins[width - 1 : width, :] - (rcv * width + channel)
     of_sources = channels - (src * width + channel) - pair_bins[:, 0:1].reshape(1, width)

time: 27.9 us -> 27.6 us (0.989)
  Pallas kernels: 10 us -> 9.57 us
  transfers between devices with their start and end apart: 10 -> 10, of which waited for: 3 -> 4; matrix products, arithmetic and copies ran while one was open for 7% -> 7% of each run, Pallas kernels for 13% -> 12%
where the time goes in v4:
time: 27.6 us; the launch traced here: 27.4 us
  starting transfers between devices  12.1 us (44%)
  Pallas kernels  9.57 us (35%)
  local copies, waits for them, and re-layouts  2.55 us (9%)
  waiting for transfers between devices  2.19 us (8%)
  other arithmetic  0.94 us (3%)
    ppermute x3, starting transfers between devices, on_device(): arrived = lax.ppermute(jitter, ('src', 'rcv'), pairs)  7.1 us
    pallas_call x1, Pallas kernels, on_device(): pl.pallas_call(functools.partial(late_kernel, width, residues, segs, leng...  6.21 us
    ppermute x3, starting transfers between devices, on_device(): lax.ppermute(mine, 'src', partners('src', k))  4.46 us
    pallas_call x1, Pallas kernels, block_spectra(): pl.pallas_call(functools.partial(block_kernel, width, residues), out_shap...  1.85 us
    unnamed x6, local copies, waits for them, and re-layouts  1.61 us
    pallas_call x1, Pallas kernels, on_device(): pl.pallas_call(functools.partial(first_kernel, fir_taps.shape[0] // 2, gr...  1.5 us
    ppermute x3, waiting for transfers between devices, on_device(): lax.ppermute(mine, 'src', partners('src', k))  1.35 us
    slice x1, local copies, waits for them, and re-layouts, on_device(): pair_bins[:, 0:1].reshape(1, width)  0.94 us
  transfers between devices with their start and end apart: 10, of which 4 were waited for; matrix products, arithmetic and copies ran while one was open for 7% of the time, Pallas kernels for 12%

profile of v4, /device:TPU:0, one launch (start us, length us, event | category | flops | bytes accessed | tf_op | source)
XLA Modules:
  0.0 27.4 jit_solution(390510509799492572)
XLA Ops:
  0.0 3.9 %collective-permute-start.4 = (bf16[256,512]{1,0:T(8,128)(2,1)}, bf16[256,512]{1,0:T(8,128)(2,1)S(1)}, u32[]{:S(2)}, u32[]{:S(2)}) collective-permute-start(bf16[256,512]{1,0:T(8,128)(2,1)} %bitcast.5), channel_id=1, source_target_pairs={{0,24},{8,16},{16,8},{24,0},{1,25},{9,17},{17,9},{25,1},{2,26},{10... | collective-permute-start | bytes 786440 | tf_op jit(solution)/shard_map/ppermute | solution.py:299
  3.9 0.5 %collective-permute-start.3 = (bf16[256,512]{1,0:T(8,128)(2,1)}, bf16[256,512]{1,0:T(8,128)(2,1)S(1)}, u32[]{:S(2)}, u32[]{:S(2)}) collective-permute-start(bf16[256,512]{1,0:T(8,128)(2,1)} %bitcast.6), channel_id=1, source_target_pairs={{0,16},{8,24},{16,0},{24,8},{1,17},{9,25},{17,1},{25,9},{2,18},{10... | collective-permute-start | bytes 786440 | tf_op jit(solution)/shard_map/ppermute | solution.py:299
  4.4 0.1 collective-permute-start.2
  4.5 0.0 collective-permute-start
  4.5 0.9 %slice_reduce_fusion = s32[128]{0:T(128)S(1)} fusion(s32[128,128]{1,0:T(8,128)} %param.6), kind=kLoop, calls=%fused_computation | loop fusion | bytes 1024 | tf_op jit(solution)/shard_map/slice | solution.py:306
  5.4 0.7 %subtract_bitcast_fusion = s32[128]{0:T(128)S(1)} fusion(s32[128,128]{1,0:T(8,128)} %param.6, s32[]{:T(128)S(6)} %mul.6), kind=kLoop, calls=%fused_computation.5 | loop fusion | flops 256 | bytes 1028 | tf_op jit(solution)/shard_map/jit(_where)/broadcast_in_dim | solution.py:308
  6.1 0.1 add_convert_fusion
  6.2 3.1 %collective-permute-start.1 = (f32[4,128]{1,0:T(4,128)S(1)}, f32[4,128]{1,0:T(4,128)S(1)}, u32[]{:S(2)}, u32[]{:S(2)}) collective-permute-start(f32[4,128]{1,0:T(4,128)S(1)} %add_convert_fusion), channel_id=1, source_target_pairs={{0,4},{2,6},{4,0},{6,2},{8,12},{10,14},{12,8},{14,10},{16,20},{18,... | collective-permute-start | bytes 6152 | tf_op jit(solution)/shard_map/ppermute | solution.py:356
  9.3 0.0 collective-permute-done.mate
  9.3 0.0 copy-start
  9.3 0.9 %copy-done = bf16[2,128,512]{2,1,0:T(8,128)(2,1)S(1)} copy-done((bf16[2,128,512]{2,1,0:T(8,128)(2,1)S(1)}, bf16[2,128,512]{2,1,0:T(8,128)(2,1)}, u32[]{:S(2)}) %copy-start) | copy-done | bytes 262168
  10.2 0.0 copy-start.2
  10.2 0.7 %copy-done.2 = bf16[31]{0:T(256)(128)(2,1)S(1)} copy-done((bf16[31]{0:T(256)(128)(2,1)S(1)}, bf16[31]{0:T(256)(128)(2,1)}, u32[]{:S(2)}) %copy-start.2) | copy-done | bytes 86
  10.9 1.5 %tables_and_own_spectra.1 = (bf16[512,512]{1,0:T(8,128)(2,1)S(1)}, bf16[576,1024]{1,0:T(8,128)(2,1)S(1)}, bf16[256,864]{1,0:T(8,128)(2,1)S(1)}, bf16[4,576,128]{2,1,0:T(8,128)(2,1)S(1)}) custom-call(bf16[1,31]{1,0:T(2,128)(2,1)S(1)} %bitcast.11, bf16[256,512]{1,0:T(8,128)(2,1)S(1)} %bitcast.9, bf16[256,512]{1,0:T(8,128)(2,1)S(1)} %collective-permute-done.mate), custom_call_target="tpu_custom_call" | custom-call | flops 10000000 | bytes 30000 | tf_op jit(solution)/shard_map/tables_and_own_spectra/pallas_call | solution.py:316
  12.4 0.0 collective-permute-done.1
  12.4 0.1 fusion
  12.5 2.5 %collective-permute-start.5 = (f32[4,128]{1,0:T(4,128)S(1)}, f32[4,128]{1,0:T(4,128)S(1)}, u32[]{:S(2)}, u32[]{:S(2)}) collective-permute-start(f32[4,128]{1,0:T(4,128)S(1)} %fusion), channel_id=1, source_target_pairs={{0,10},{2,8},{4,14},{6,12},{8,2},{10,0},{12,6},{14,4},{16,26},{18,... | collective-permute-start | bytes 6152 | tf_op jit(solution)/shard_map/ppermute | solution.py:356
  15.0 0.0 collective-permute-done.4.refs_5_
  15.0 1.0 %collective-permute-done.3.refs_1_ = bf16[256,512]{1,0:T(8,128)(2,1)S(1)} collective-permute-done((bf16[256,512]{1,0:T(8,128)(2,1)}, bf16[256,512]{1,0:T(8,128)(2,1)S(1)}, u32[]{:S(2)}, u32[]{:S(2)}) %collective-permute-start.3) | collective-permute-done | bytes 262176 | tf_op jit(solution)/shard_map/ppermute | solution.py:299
  16.0 0.3 %collective-permute-done.2.refs_0_ = bf16[256,512]{1,0:T(8,128)(2,1)S(1)} collective-permute-done((bf16[256,512]{1,0:T(8,128)(2,1)}, bf16[256,512]{1,0:T(8,128)(2,1)S(1)}, u32[]{:S(2)}, u32[]{:S(2)}) %collective-permute-start.2) | collective-permute-done | bytes 262176 | tf_op jit(solution)/shard_map/ppermute | solution.py:299
  16.3 0.6 %collective-permute-done.5 = f32[4,128]{1,0:T(4,128)S(1)} collective-permute-done((f32[4,128]{1,0:T(4,128)S(1)}, f32[4,128]{1,0:T(4,128)S(1)}, u32[]{:S(2)}, u32[]{:S(2)}) %collective-permute-start.5) | collective-permute-done | bytes 2080 | tf_op jit(solution)/shard_map/ppermute | solution.py:356
  17.0 0.0 collective-permute-start.7
  17.0 0.5 %collective-permute-start.8 = (bf16[256,512]{1,0:T(8,128)(2,1)S(1)}, bf16[256,512]{1,0:T(8,128)(2,1)S(1)}, u32[]{:S(2)}, u32[]{:S(2)}) collective-permute-start(bf16[256,512]{1,0:T(8,128)(2,1)S(1)} %collective-permute-done.3.refs_1_), channel_id=1, source_target_pairs={{0,1},{1,0},{2,3},{3,2},{4,5},{5,4},{6,7},{7,6},{8,9},{9,8},{10,11... | collective-permute-start | bytes 786440 | tf_op jit(solution)/shard_map/ppermute | solution.py:297
  17.5 0.0 collective-permute-start.9
  17.5 0.1 fusion.1.refs_0_
  17.6 1.5 %collective-permute-start.6 = (f32[4,128]{1,0:T(4,128)S(1)}, f32[4,128]{1,0:T(4,128)S(1)}, u32[]{:S(2)}, u32[]{:S(2)}) collective-permute-start(f32[4,128]{1,0:T(4,128)S(1)} %fusion.1.refs_0_), channel_id=1, source_target_pairs={{0,16},{2,18},{4,20},{6,22},{8,24},{10,26},{12,28},{14,30},{16,0},... | collective-permute-start | bytes 6152 | tf_op jit(solution)/shard_map/ppermute | solution.py:356
  19.1 0.0 collective-permute-done.7.refs_2_
  19.1 0.0 collective-permute-done.8.refs_3_
  19.1 0.0 copy-start.1
  19.1 1.9 %block_spectra.1 = (bf16[4,576,128]{2,1,0:T(8,128)(2,1)S(1)}, bf16[4,576,128]{2,1,0:T(8,128)(2,1)S(1)}) custom-call(bf16[512,512]{1,0:T(8,128)(2,1)S(1)} %get-tuple-element.18.matrix_t, bf16[576,1024]{1,0:T(8,128)(2,1)S(1)} %get-tuple-element.19.table, bf16[256,512]{1,0:T(8,128)(2,1)S(1)} %collective-permute-done.2.refs_0_, ...), custom_call_target="tpu_custom_call" | custom-call | flops 10000000 | bytes 30000 | tf_op jit(solution)/shard_map/block_spectra/pallas_call | solution.py:332
  21.0 0.2 collective-permute-done.6.refs_1_
  21.2 0.0 collective-permute-done.9.refs_6_
  21.2 0.0 copy-done.1
  21.2 6.2 %bin_stacks.1 = f32[32,128]{1,0:T(8,128)} custom-call(s32[8,128]{1,0:T(8,128)S(1)} %bitcast.10, bf16[512,512]{1,0:T(8,128)(2,1)S(1)} %get-tuple-element.18.matrix_t, bf16[576,1024]{1,0:T(8,128)(2,1)S(1)} %get-tuple-element.19.table, bf16[256,864]{1,0:T(8,128)(2,1)S(1)} %get-tuple-element.20.inverse, f32[4,128]{1,0:T(4,128)S(1)} %fusion.1.refs_0_, ...), custom_call_target="tpu_custom_call" | custom-call | flops 10000000 | bytes 30000 | tf_op jit(solution)/shard_map/bin_stacks/pallas_call | solution.py:360
  (2 shorter events, 0.0 us)
Async XLA Ops:
  0.0 15.0 %collective-permute-start.4 = (bf16[256,512]{1,0:T(8,128)(2,1)}, bf16[256,512]{1,0:T(8,128)(2,1)S(1)}, u32[]{:S(2)}, u32[]{:S(2)}) collective-permute-start(bf16[256,512]{1,0:T(8,128)(2,1)} %bitcast.5), channel_id=1, source_target_pairs={{0,24},{8,16},{16,8},{24,0},{1,25},{9,17},{17,9},{25,1},{2,26},{10... | collective-permute-start | bytes 786440 | tf_op jit(solution)/shard_map/ppermute | solution.py:299
  3.9 12.1 %collective-permute-start.3 = (bf16[256,512]{1,0:T(8,128)(2,1)}, bf16[256,512]{1,0:T(8,128)(2,1)S(1)}, u32[]{:S(2)}, u32[]{:S(2)}) collective-permute-start(bf16[256,512]{1,0:T(8,128)(2,1)} %bitcast.6), channel_id=1, source_target_pairs={{0,16},{8,24},{16,0},{24,8},{1,17},{9,25},{17,1},{25,9},{2,18},{10... | collective-permute-start | bytes 786440 | tf_op jit(solution)/shard_map/ppermute | solution.py:299
  4.4 11.9 %collective-permute-start.2 = (bf16[256,512]{1,0:T(8,128)(2,1)}, bf16[256,512]{1,0:T(8,128)(2,1)S(1)}, u32[]{:S(2)}, u32[]{:S(2)}) collective-permute-start(bf16[256,512]{1,0:T(8,128)(2,1)} %bitcast.7), channel_id=1, source_target_pairs={{0,8},{8,0},{16,24},{24,16},{1,9},{9,1},{17,25},{25,17},{2,10},{10... | collective-permute-start | bytes 786440 | tf_op jit(solution)/shard_map/ppermute | solution.py:299
  4.5 4.8 %collective-permute-start = (bf16[256,512]{1,0:T(8,128)(2,1)}, bf16[256,512]{1,0:T(8,128)(2,1)S(1)}, u32[]{:S(2)}, u32[]{:S(2)}) collective-permute-start(bf16[256,512]{1,0:T(8,128)(2,1)} %bitcast.8), channel_id=1, source_target_pairs={{0,1},{1,0},{2,3},{3,2},{4,5},{5,4},{6,7},{7,6},{8,9},{9,8},{10,11... | collective-permute-start | bytes 786440 | tf_op jit(solution)/shard_map/ppermute | solution.py:297
  6.2 6.2 %collective-permute-start.1 = (f32[4,128]{1,0:T(4,128)S(1)}, f32[4,128]{1,0:T(4,128)S(1)}, u32[]{:S(2)}, u32[]{:S(2)}) collective-permute-start(f32[4,128]{1,0:T(4,128)S(1)} %add_convert_fusion), channel_id=1, source_target_pairs={{0,4},{2,6},{4,0},{6,2},{8,12},{10,14},{12,8},{14,10},{16,20},{18,... | collective-permute-start | bytes 6152 | tf_op jit(solution)/shard_map/ppermute | solution.py:356
  9.3 1.0 %copy-start = (bf16[2,128,512]{2,1,0:T(8,128)(2,1)S(1)}, bf16[2,128,512]{2,1,0:T(8,128)(2,1)}, u32[]{:S(2)}) copy-start(bf16[2,128,512]{2,1,0:T(8,128)(2,1)} %param.4) | copy-start | bytes 786436
  10.2 0.7 %copy-start.2 = (bf16[31]{0:T(256)(128)(2,1)S(1)}, bf16[31]{0:T(256)(128)(2,1)}, u32[]{:S(2)}) copy-start(bf16[31]{0:T(256)(128)(2,1)} %param.5) | copy-start | bytes 190
  12.5 4.5 %collective-permute-start.5 = (f32[4,128]{1,0:T(4,128)S(1)}, f32[4,128]{1,0:T(4,128)S(1)}, u32[]{:S(2)}, u32[]{:S(2)}) collective-permute-start(f32[4,128]{1,0:T(4,128)S(1)} %fusion), channel_id=1, source_target_pairs={{0,10},{2,8},{4,14},{6,12},{8,2},{10,0},{12,6},{14,4},{16,26},{18,... | collective-permute-start | bytes 6152 | tf_op jit(solution)/shard_map/ppermute | solution.py:356
  17.0 2.1 %collective-permute-start.7 = (bf16[256,512]{1,0:T(8,128)(2,1)S(1)}, bf16[256,512]{1,0:T(8,128)(2,1)S(1)}, u32[]{:S(2)}, u32[]{:S(2)}) collective-permute-start(bf16[256,512]{1,0:T(8,128)(2,1)S(1)} %collective-permute-done.2.refs_0_), channel_id=1, source_target_pairs={{0,1},{1,0},{2,3},{3,2},{4,5},{5,4},{6,7},{7,6},{8,9},{9,8},{10,11... | collective-permute-start | bytes 786440 | tf_op jit(solution)/shard_map/ppermute | solution.py:297
  17.0 2.1 %collective-permute-start.8 = (bf16[256,512]{1,0:T(8,128)(2,1)S(1)}, bf16[256,512]{1,0:T(8,128)(2,1)S(1)}, u32[]{:S(2)}, u32[]{:S(2)}) collective-permute-start(bf16[256,512]{1,0:T(8,128)(2,1)S(1)} %collective-permute-done.3.refs_1_), channel_id=1, source_target_pairs={{0,1},{1,0},{2,3},{3,2},{4,5},{5,4},{6,7},{7,6},{8,9},{9,8},{10,11... | collective-permute-start | bytes 786440 | tf_op jit(solution)/shard_map/ppermute | solution.py:297
  17.5 3.7 %collective-permute-start.9 = (bf16[256,512]{1,0:T(8,128)(2,1)S(1)}, bf16[256,512]{1,0:T(8,128)(2,1)S(1)}, u32[]{:S(2)}, u32[]{:S(2)}) collective-permute-start(bf16[256,512]{1,0:T(8,128)(2,1)S(1)} %collective-permute-done.4.refs_5_), channel_id=1, source_target_pairs={{0,1},{1,0},{2,3},{3,2},{4,5},{5,4},{6,7},{7,6},{8,9},{9,8},{10,11... | collective-permute-start | bytes 786440 | tf_op jit(solution)/shard_map/ppermute | solution.py:297
  17.6 3.6 %collective-permute-start.6 = (f32[4,128]{1,0:T(4,128)S(1)}, f32[4,128]{1,0:T(4,128)S(1)}, u32[]{:S(2)}, u32[]{:S(2)}) collective-permute-start(f32[4,128]{1,0:T(4,128)S(1)} %fusion.1.refs_0_), channel_id=1, source_target_pairs={{0,16},{2,18},{4,20},{6,22},{8,24},{10,26},{12,28},{14,30},{16,0},... | collective-permute-start | bytes 6152 | tf_op jit(solution)/shard_map/ppermute | solution.py:356
  19.1 2.1 %copy-start.1 = (s32[1024]{0:T(1024)S(1)}, s32[1024]{0:T(1024)}, u32[]{:S(2)}) copy-start(s32[1024]{0:T(1024)} %param.7) | copy-start | bytes 12292

commit v5 on v4

--- a/solution.py
+++ b/solution.py
@@ -102,7 +102,9 @@
     filtered = jnp.concatenate(
         [early[0:start], early[start:stop] + late[0 : 2 * BAND], late[2 * BAND :]], 0
     ).astype(BF16)
-    return dot(table, jnp.concatenate([filtered, filtered], 0)).astype(BF16)
+    length, height = filtered.shape[0], table.shape[0]
+    halves = dot(jnp.concatenate([table[:, 0:length], table[:, length:]], 0), filtered)
+    return (halves[0:height] + halves[height:]).astype(BF16)
 
 
 def block_kernel(width, residues, matrix_t, table, *refs):

time: 27.6 us -> 27.5 us (level)
  no operation moved by 1% of the time
where the time goes in v5:
time: 27.5 us; the launch traced here: 27.3 us
  starting transfers between devices  12.1 us (44%)
  Pallas kernels  9.51 us (35%)
  local copies, waits for them, and re-layouts  2.55 us (9%)
  waiting for transfers between devices  2.19 us (8%)
  other arithmetic  0.94 us (3%)
    ppermute x3, starting transfers between devices, on_device(): arrived = lax.ppermute(jitter, ('src', 'rcv'), pairs)  7.1 us
    pallas_call x1, Pallas kernels, on_device(): pl.pallas_call(functools.partial(late_kernel, width, residues, segs, leng...  6.22 us
    ppermute x3, starting transfers between devices, on_device(): lax.ppermute(mine, 'src', partners('src', k))  4.46 us
    pallas_call x1, Pallas kernels, block_spectra(): pl.pallas_call(functools.partial(block_kernel, width, residues), out_shap...  1.85 us
    unnamed x6, local copies, waits for them, and re-layouts  1.61 us
    pallas_call x1, Pallas kernels, on_device(): pl.pallas_call(functools.partial(first_kernel, fir_taps.shape[0] // 2, gr...  1.44 us
    ppermute x3, waiting for transfers between devices, on_device(): lax.ppermute(mine, 'src', partners('src', k))  1.41 us
    slice x1, local copies, waits for them, and re-layouts, on_device(): pair_bins[:, 0:1].reshape(1, width)  0.94 us
  transfers between devices with their start and end apart: 10, of which 4 were waited for; matrix products, arithmetic and copies ran while one was open for 7% of the time, Pallas kernels for 12%

profile of v5, /device:TPU:0, one launch (start us, length us, event | category | flops | bytes accessed | tf_op | source)
XLA Modules:
  0.0 27.3 jit_solution(10927666293212253592)
XLA Ops:
  0.0 3.9 %collective-permute-start.4 = (bf16[256,512]{1,0:T(8,128)(2,1)}, bf16[256,512]{1,0:T(8,128)(2,1)S(1)}, u32[]{:S(2)}, u32[]{:S(2)}) collective-permute-start(bf16[256,512]{1,0:T(8,128)(2,1)} %bitcast.5), channel_id=1, source_target_pairs={{0,24},{8,16},{16,8},{24,0},{1,25},{9,17},{17,9},{25,1},{2,26},{10... | collective-permute-start | bytes 786440 | tf_op jit(solution)/shard_map/ppermute | solution.py:301
  3.9 0.5 %collective-permute-start.3 = (bf16[256,512]{1,0:T(8,128)(2,1)}, bf16[256,512]{1,0:T(8,128)(2,1)S(1)}, u32[]{:S(2)}, u32[]{:S(2)}) collective-permute-start(bf16[256,512]{1,0:T(8,128)(2,1)} %bitcast.6), channel_id=1, source_target_pairs={{0,16},{8,24},{16,0},{24,8},{1,17},{9,25},{17,1},{25,9},{2,18},{10... | collective-permute-start | bytes 786440 | tf_op jit(solution)/shard_map/ppermute | solution.py:301
  4.4 0.1 collective-permute-start.2
  4.5 0.0 collective-permute-start
  4.5 0.9 %slice_reduce_fusion = s32[128]{0:T(128)S(1)} fusion(s32[128,128]{1,0:T(8,128)} %param.6), kind=kLoop, calls=%fused_computation | loop fusion | bytes 1024 | tf_op jit(solution)/shard_map/slice | solution.py:308
  5.4 0.7 %subtract_bitcast_fusion = s32[128]{0:T(128)S(1)} fusion(s32[128,128]{1,0:T(8,128)} %param.6, s32[]{:T(128)S(6)} %mul.6), kind=kLoop, calls=%fused_computation.5 | loop fusion | flops 256 | bytes 1028 | tf_op jit(solution)/shard_map/jit(_where)/broadcast_in_dim | solution.py:310
  6.1 0.1 add_convert_fusion
  6.2 3.1 %collective-permute-start.1 = (f32[4,128]{1,0:T(4,128)S(1)}, f32[4,128]{1,0:T(4,128)S(1)}, u32[]{:S(2)}, u32[]{:S(2)}) collective-permute-start(f32[4,128]{1,0:T(4,128)S(1)} %add_convert_fusion), channel_id=1, source_target_pairs={{0,4},{2,6},{4,0},{6,2},{8,12},{10,14},{12,8},{14,10},{16,20},{18,... | collective-permute-start | bytes 6152 | tf_op jit(solution)/shard_map/ppermute | solution.py:358
  9.3 0.0 collective-permute-done.mate
  9.3 0.0 copy-start
  9.3 0.9 %copy-done = bf16[2,128,512]{2,1,0:T(8,128)(2,1)S(1)} copy-done((bf16[2,128,512]{2,1,0:T(8,128)(2,1)S(1)}, bf16[2,128,512]{2,1,0:T(8,128)(2,1)}, u32[]{:S(2)}) %copy-start) | copy-done | bytes 262168
  10.2 0.0 copy-start.2
  10.2 0.7 %copy-done.2 = bf16[31]{0:T(256)(128)(2,1)S(1)} copy-done((bf16[31]{0:T(256)(128)(2,1)S(1)}, bf16[31]{0:T(256)(128)(2,1)}, u32[]{:S(2)}) %copy-start.2) | copy-done | bytes 86
  10.9 1.4 %tables_and_own_spectra.1 = (bf16[512,512]{1,0:T(8,128)(2,1)S(1)}, bf16[576,1024]{1,0:T(8,128)(2,1)S(1)}, bf16[256,864]{1,0:T(8,128)(2,1)S(1)}, bf16[4,576,128]{2,1,0:T(8,128)(2,1)S(1)}) custom-call(bf16[1,31]{1,0:T(2,128)(2,1)S(1)} %bitcast.11, bf16[256,512]{1,0:T(8,128)(2,1)S(1)} %bitcast.9, bf16[256,512]{1,0:T(8,128)(2,1)S(1)} %collective-permute-done.mate), custom_call_target="tpu_custom_call" | custom-call | flops 10000000 | bytes 30000 | tf_op jit(solution)/shard_map/tables_and_own_spectra/pallas_call | solution.py:318
  12.3 0.0 collective-permute-done.1
  12.3 0.1 fusion
  12.4 2.5 %collective-permute-start.5 = (f32[4,128]{1,0:T(4,128)S(1)}, f32[4,128]{1,0:T(4,128)S(1)}, u32[]{:S(2)}, u32[]{:S(2)}) collective-permute-start(f32[4,128]{1,0:T(4,128)S(1)} %fusion), channel_id=1, source_target_pairs={{0,10},{2,8},{4,14},{6,12},{8,2},{10,0},{12,6},{14,4},{16,26},{18,... | collective-permute-start | bytes 6152 | tf_op jit(solution)/shard_map/ppermute | solution.py:358
  14.9 0.0 collective-permute-done.4.refs_5_
  14.9 1.1 %collective-permute-done.3.refs_1_ = bf16[256,512]{1,0:T(8,128)(2,1)S(1)} collective-permute-done((bf16[256,512]{1,0:T(8,128)(2,1)}, bf16[256,512]{1,0:T(8,128)(2,1)S(1)}, u32[]{:S(2)}, u32[]{:S(2)}) %collective-permute-start.3) | collective-permute-done | bytes 262176 | tf_op jit(solution)/shard_map/ppermute | solution.py:301
  16.0 0.3 %collective-permute-done.2.refs_0_ = bf16[256,512]{1,0:T(8,128)(2,1)S(1)} collective-permute-done((bf16[256,512]{1,0:T(8,128)(2,1)}, bf16[256,512]{1,0:T(8,128)(2,1)S(1)}, u32[]{:S(2)}, u32[]{:S(2)}) %collective-permute-start.2) | collective-permute-done | bytes 262176 | tf_op jit(solution)/shard_map/ppermute | solution.py:301
  16.3 0.6 %collective-permute-done.5 = f32[4,128]{1,0:T(4,128)S(1)} collective-permute-done((f32[4,128]{1,0:T(4,128)S(1)}, f32[4,128]{1,0:T(4,128)S(1)}, u32[]{:S(2)}, u32[]{:S(2)}) %collective-permute-start.5) | collective-permute-done | bytes 2080 | tf_op jit(solution)/shard_map/ppermute | solution.py:358
  16.9 0.0 collective-permute-start.7
  16.9 0.5 %collective-permute-start.8 = (bf16[256,512]{1,0:T(8,128)(2,1)S(1)}, bf16[256,512]{1,0:T(8,128)(2,1)S(1)}, u32[]{:S(2)}, u32[]{:S(2)}) collective-permute-start(bf16[256,512]{1,0:T(8,128)(2,1)S(1)} %collective-permute-done.3.refs_1_), channel_id=1, source_target_pairs={{0,1},{1,0},{2,3},{3,2},{4,5},{5,4},{6,7},{7,6},{8,9},{9,8},{10,11... | collective-permute-start | bytes 786440 | tf_op jit(solution)/shard_map/ppermute | solution.py:299
  17.4 0.0 collective-permute-start.9
  17.4 0.1 fusion.1.refs_0_
  17.5 1.5 %collective-permute-start.6 = (f32[4,128]{1,0:T(4,128)S(1)}, f32[4,128]{1,0:T(4,128)S(1)}, u32[]{:S(2)}, u32[]{:S(2)}) collective-permute-start(f32[4,128]{1,0:T(4,128)S(1)} %fusion.1.refs_0_), channel_id=1, source_target_pairs={{0,16},{2,18},{4,20},{6,22},{8,24},{10,26},{12,28},{14,30},{16,0},... | collective-permute-start | bytes 6152 | tf_op jit(solution)/shard_map/ppermute | solution.py:358
  19.0 0.0 collective-permute-done.7.refs_2_
  19.0 0.0 collective-permute-done.8.refs_3_
  19.0 0.0 copy-start.1
  19.0 1.9 %block_spectra.1 = (bf16[4,576,128]{2,1,0:T(8,128)(2,1)S(1)}, bf16[4,576,128]{2,1,0:T(8,128)(2,1)S(1)}) custom-call(bf16[512,512]{1,0:T(8,128)(2,1)S(1)} %get-tuple-element.18.matrix_t, bf16[576,1024]{1,0:T(8,128)(2,1)S(1)} %get-tuple-element.19.table, bf16[256,512]{1,0:T(8,128)(2,1)S(1)} %collective-permute-done.2.refs_0_, ...), custom_call_target="tpu_custom_call" | custom-call | flops 10000000 | bytes 30000 | tf_op jit(solution)/shard_map/block_spectra/pallas_call | solution.py:334
  20.9 0.2 collective-permute-done.6.refs_1_
  21.1 0.0 collective-permute-done.9.refs_6_
  21.1 0.0 copy-done.1
  21.1 6.2 %bin_stacks.1 = f32[32,128]{1,0:T(8,128)} custom-call(s32[8,128]{1,0:T(8,128)S(1)} %bitcast.10, bf16[512,512]{1,0:T(8,128)(2,1)S(1)} %get-tuple-element.18.matrix_t, bf16[576,1024]{1,0:T(8,128)(2,1)S(1)} %get-tuple-element.19.table, bf16[256,864]{1,0:T(8,128)(2,1)S(1)} %get-tuple-element.20.inverse, f32[4,128]{1,0:T(4,128)S(1)} %fusion.1.refs_0_, ...), custom_call_target="tpu_custom_call" | custom-call | flops 10000000 | bytes 30000 | tf_op jit(solution)/shard_map/bin_stacks/pallas_call | solution.py:362
  (2 shorter events, 0.0 us)
Async XLA Ops:
  0.0 14.9 %collective-permute-start.4 = (bf16[256,512]{1,0:T(8,128)(2,1)}, bf16[256,512]{1,0:T(8,128)(2,1)S(1)}, u32[]{:S(2)}, u32[]{:S(2)}) collective-permute-start(bf16[256,512]{1,0:T(8,128)(2,1)} %bitcast.5), channel_id=1, source_target_pairs={{0,24},{8,16},{16,8},{24,0},{1,25},{9,17},{17,9},{25,1},{2,26},{10... | collective-permute-start | bytes 786440 | tf_op jit(solution)/shard_map/ppermute | solution.py:301
  3.9 12.1 %collective-permute-start.3 = (bf16[256,512]{1,0:T(8,128)(2,1)}, bf16[256,512]{1,0:T(8,128)(2,1)S(1)}, u32[]{:S(2)}, u32[]{:S(2)}) collective-permute-start(bf16[256,512]{1,0:T(8,128)(2,1)} %bitcast.6), channel_id=1, source_target_pairs={{0,16},{8,24},{16,0},{24,8},{1,17},{9,25},{17,1},{25,9},{2,18},{10... | collective-permute-start | bytes 786440 | tf_op jit(solution)/shard_map/ppermute | solution.py:301
  4.4 11.9 %collective-permute-start.2 = (bf16[256,512]{1,0:T(8,128)(2,1)}, bf16[256,512]{1,0:T(8,128)(2,1)S(1)}, u32[]{:S(2)}, u32[]{:S(2)}) collective-permute-start(bf16[256,512]{1,0:T(8,128)(2,1)} %bitcast.7), channel_id=1, source_target_pairs={{0,8},{8,0},{16,24},{24,16},{1,9},{9,1},{17,25},{25,17},{2,10},{10... | collective-permute-start | bytes 786440 | tf_op jit(solution)/shard_map/ppermute | solution.py:301
  4.5 4.8 %collective-permute-start = (bf16[256,512]{1,0:T(8,128)(2,1)}, bf16[256,512]{1,0:T(8,128)(2,1)S(1)}, u32[]{:S(2)}, u32[]{:S(2)}) collective-permute-start(bf16[256,512]{1,0:T(8,128)(2,1)} %bitcast.8), channel_id=1, source_target_pairs={{0,1},{1,0},{2,3},{3,2},{4,5},{5,4},{6,7},{7,6},{8,9},{9,8},{10,11... | collective-permute-start | bytes 786440 | tf_op jit(solution)/shard_map/ppermute | solution.py:299
  6.2 6.1 %collective-permute-start.1 = (f32[4,128]{1,0:T(4,128)S(1)}, f32[4,128]{1,0:T(4,128)S(1)}, u32[]{:S(2)}, u32[]{:S(2)}) collective-permute-start(f32[4,128]{1,0:T(4,128)S(1)} %add_convert_fusion), channel_id=1, source_target_pairs={{0,4},{2,6},{4,0},{6,2},{8,12},{10,14},{12,8},{14,10},{16,20},{18,... | collective-permute-start | bytes 6152 | tf_op jit(solution)/shard_map/ppermute | solution.py:358
  9.3 1.0 %copy-start = (bf16[2,128,512]{2,1,0:T(8,128)(2,1)S(1)}, bf16[2,128,512]{2,1,0:T(8,128)(2,1)}, u32[]{:S(2)}) copy-start(bf16[2,128,512]{2,1,0:T(8,128)(2,1)} %param.4) | copy-start | bytes 786436
  10.2 0.7 %copy-start.2 = (bf16[31]{0:T(256)(128)(2,1)S(1)}, bf16[31]{0:T(256)(128)(2,1)}, u32[]{:S(2)}) copy-start(bf16[31]{0:T(256)(128)(2,1)} %param.5) | copy-start | bytes 190
  12.4 4.5 %collective-permute-start.5 = (f32[4,128]{1,0:T(4,128)S(1)}, f32[4,128]{1,0:T(4,128)S(1)}, u32[]{:S(2)}, u32[]{:S(2)}) collective-permute-start(f32[4,128]{1,0:T(4,128)S(1)} %fusion), channel_id=1, source_target_pairs={{0,10},{2,8},{4,14},{6,12},{8,2},{10,0},{12,6},{14,4},{16,26},{18,... | collective-permute-start | bytes 6152 | tf_op jit(solution)/shard_map/ppermute | solution.py:358
  16.9 2.1 %collective-permute-start.7 = (bf16[256,512]{1,0:T(8,128)(2,1)S(1)}, bf16[256,512]{1,0:T(8,128)(2,1)S(1)}, u32[]{:S(2)}, u32[]{:S(2)}) collective-permute-start(bf16[256,512]{1,0:T(8,128)(2,1)S(1)} %collective-permute-done.2.refs_0_), channel_id=1, source_target_pairs={{0,1},{1,0},{2,3},{3,2},{4,5},{5,4},{6,7},{7,6},{8,9},{9,8},{10,11... | collective-permute-start | bytes 786440 | tf_op jit(solution)/shard_map/ppermute | solution.py:299
  16.9 2.1 %collective-permute-start.8 = (bf16[256,512]{1,0:T(8,128)(2,1)S(1)}, bf16[256,512]{1,0:T(8,128)(2,1)S(1)}, u32[]{:S(2)}, u32[]{:S(2)}) collective-permute-start(bf16[256,512]{1,0:T(8,128)(2,1)S(1)} %collective-permute-done.3.refs_1_), channel_id=1, source_target_pairs={{0,1},{1,0},{2,3},{3,2},{4,5},{5,4},{6,7},{7,6},{8,9},{9,8},{10,11... | collective-permute-start | bytes 786440 | tf_op jit(solution)/shard_map/ppermute | solution.py:299
  17.4 3.7 %collective-permute-start.9 = (bf16[256,512]{1,0:T(8,128)(2,1)S(1)}, bf16[256,512]{1,0:T(8,128)(2,1)S(1)}, u32[]{:S(2)}, u32[]{:S(2)}) collective-permute-start(bf16[256,512]{1,0:T(8,128)(2,1)S(1)} %collective-permute-done.4.refs_5_), channel_id=1, source_target_pairs={{0,1},{1,0},{2,3},{3,2},{4,5},{5,4},{6,7},{7,6},{8,9},{9,8},{10,11... | collective-permute-start | bytes 786440 | tf_op jit(solution)/shard_map/ppermute | solution.py:299
  17.5 3.6 %collective-permute-start.6 = (f32[4,128]{1,0:T(4,128)S(1)}, f32[4,128]{1,0:T(4,128)S(1)}, u32[]{:S(2)}, u32[]{:S(2)}) collective-permute-start(f32[4,128]{1,0:T(4,128)S(1)} %fusion.1.refs_0_), channel_id=1, source_target_pairs={{0,16},{2,18},{4,20},{6,22},{8,24},{10,26},{12,28},{14,30},{16,0},... | collective-permute-start | bytes 6152 | tf_op jit(solution)/shard_map/ppermute | solution.py:358
  19.0 2.1 %copy-start.1 = (s32[1024]{0:T(1024)S(1)}, s32[1024]{0:T(1024)}, u32[]{:S(2)}) copy-start(s32[1024]{0:T(1024)} %param.7) | copy-start | bytes 12292
